TPU v7x, 32 devices: a whole 2x2x4 slice. The times are simulated.
32 devices in a mesh: rows: 4 (over z), cols: 8 (over y, x, core).
Axes of the slice: x: 2, y: 2, z: 4, core: 2. Of those that a mesh axis runs over, the one named last changes fastest.
Arguments:
- tile_values: bfloat16 [4, 8, 4, 128, 128], P('rows', 'cols'), may hold values from 0.0009994507 to 0.019897461
- tile_rows: int32 [4, 8, 4], P('rows', 'cols'), may hold values from 0 to 7, as said below
- tile_cols: int32 [4, 8, 4], P('rows', 'cols'), may hold values from 0 to 3, as said below
- live_counts: int32 [4, 8], P('rows', 'cols'), may hold values from 1 to 4, as said below
- test_block: float32 [4096, 512], P('cols'), may hold values from -6 to 6
Outputs:
- y_sample: float32 [4096, 512], P(('rows', 'cols'))
- z_power: float32 [4096, 512], P('cols')
- panel_gram: float32 [4, 512, 512], P('rows')
Inputs may be any that keep to these rules, and one draw needn't show every extreme that they name: Within one device the pairs (tile_rows, tile_cols) of its slots are distinct. `tile_cols`: column block of a slot within the device's columns. `live_counts`: some device uses all 4 slots.
All inputs are finite; a program needn't handle non-finite values.
Results may differ from a plain program's by a relative error of at most 0.0003.
Values sent between devices are 32-bit elements; how exact they have to be, the bound alone decides.
A program may use at most 64 MiB of HBM per device.

v0:
```python
import jax
import jax.numpy as jnp
from jax import lax
from jax.sharding import PartitionSpec as P

RB_DEV = 8
CB_DEV = 4


def local(tile_values, tile_rows, tile_cols, live_counts, test_block):
    high = lax.Precision.HIGHEST
    tile_data = tile_values[0, 0]
    rows_local = tile_rows[0, 0]
    cols_local = tile_cols[0, 0]
    live_count = live_counts[0, 0]
    slots_here = tile_data.shape[0]
    test_cols = test_block.shape[1]
    keep_mask = (jnp.arange(slots_here, dtype=jnp.int32) < live_count).astype(jnp.float32)
    tiles_f = tile_data.astype(jnp.float32)
    picked = test_block.reshape(CB_DEV, 128, test_cols)[cols_local]
    products = jnp.einsum("sab,sbk->sak", tiles_f, picked, precision=high)
    row_onehot = (rows_local[:, None] == jnp.arange(RB_DEV, dtype=jnp.int32)[None, :]).astype(
        jnp.float32
    ) * keep_mask[:, None]
    partial_value = jnp.einsum("sr,sak->rak", row_onehot, products, precision=high).reshape(
        RB_DEV * 128, test_cols
    )
    y_shard = lax.psum_scatter(partial_value, "cols", scatter_dimension=0, tiled=True)
    local_gram = jnp.dot(y_shard.T, y_shard, precision=high, preferred_element_type=jnp.float32)
    gram = lax.psum(local_gram, "cols") / (RB_DEV * 128)
    y_panel = lax.all_gather(y_shard, "cols", axis=0, tiled=True)
    y_tiles = y_panel.reshape(RB_DEV, 128, test_cols)[rows_local]
    z_terms = jnp.einsum("sab,sak->sbk", tiles_f, y_tiles, precision=high)
    col_onehot = (cols_local[:, None] == jnp.arange(CB_DEV, dtype=jnp.int32)[None, :]).astype(
        jnp.float32
    ) * keep_mask[:, None]
    z_local = jnp.einsum("sc,sbk->cbk", col_onehot, z_terms, precision=high).reshape(
        CB_DEV * 128, test_cols
    )
    z_power = lax.psum(z_local, "rows")
    return (y_shard, z_power, gram[None])


def solution(mesh):
    return jax.shard_map(
        local,
        mesh=mesh,
        in_specs=(
            P("rows", "cols", None, None, None),
            P("rows", "cols", None),
            P("rows", "cols", None),
            P("rows", "cols"),
            P("cols", None),
        ),
        out_specs=(P(("rows", "cols"), None), P("cols", None), P("rows", None, None)),
        check_vma=False,
    )
```

profile of v0, /device:TPU:0, one launch (start us, length us, event | category | flops | bytes accessed | tf_op | source)
XLA Modules:
  0.0 213.7 jit_solution(3124730387253257115)
XLA Ops:
  7.2 0.0 copy-start
  7.2 0.0 copy-start.1
  7.2 0.0 reduce-scatter.2.cloned.1.call-start
  8.0 0.7 fusion.18
  8.6 0.0 copy-done
  8.7 0.6 gather_fusion
  9.3 0.0 copy-done.1
  9.3 0.0 copy-start.2
  9.3 1.0 fusion.6
  10.3 0.5 copy.10
  10.8 0.0 copy-done.2
  10.8 2.3 %fusion.2 = f32[8,128,512]{2,0,1:T(8,128)S(1)} fusion(f32[4,512,128]{1,0,2:T(4,128)S(1)} %copy.10, f32[4]{0:T(128)S(1)} %compare_convert_fusion, s32[4]{0:T(128)S(1)} %bitcast.43), kind=kOutput, calls=%fused_computation.4 | convolution fusion | flops 25165888 | bytes 3145760 | tf_op jit(solution)/shard_map/sr,sak->rak/dot_general | solution.py:25
  13.2 2.6 %copy.8 = f32[8,128,512]{2,1,0:T(8,128)} copy(f32[8,128,512]{2,0,1:T(8,128)S(1)} %fusion.2) | data formatting | bytes 4194304 | tf_op jit(solution)/shard_map/sr,sak->rak/dot_general | solution.py:25
  15.7 0.0 reduce-scatter.2.cloned.1.call-update
  15.7 0.0 all-gather.2.cloned.1.call-start
  15.8 44.0 %reduce-scatter.2.cloned.1.call-done = f32[128,512]{1,0:T(8,128)} async-done(((f32[1024,512]{1,0:T(8,128)}), f32[128,512]{1,0:T(8,128)}) %reduce-scatter.2.cloned.1.call-update) | async-done | bytes 262160 | tf_op jit(solution)/shard_map/reduce_scatter | solution.py:28
  59.8 0.0 all-gather.2.cloned.1.call-update
  59.8 0.0 all-reduce.5.cloned.1.call-start
  59.9 3.0 %fusion.22 = f32[512,512]{1,0:T(8,128)} fusion(f32[128,512]{1,0:T(8,128)} %reduce-scatter.2.cloned.1.call-done), kind=kOutput, calls=%fused_computation.32 | convolution fusion | flops 402653184 | bytes 1310720 | tf_op jit(solution)/shard_map/dot_general | solution.py:29
  62.9 0.0 all-reduce.5.cloned.1.call-update
  62.9 0.0 all-reduce.3.cloned.1.call-start
  63.0 27.4 %all-gather.2.cloned.1.call-done = f32[1024,512]{1,0:T(8,128)} async-done(((f32[128,512]{1,0:T(8,128)}), f32[1024,512]{1,0:T(8,128)}) %all-gather.2.cloned.1.call-update) | async-done | bytes 2097168 | tf_op jit(solution)/shard_map/all_gather | solution.py:31
  90.4 2.2 %gather_fusion.1 = f32[4,128,512]{2,1,0:T(8,128)S(1)} fusion(f32[8,128,512]{2,1,0:T(8,128)} %bitcast.42, s32[1024]{0:T(1024)S(1)} %pad_clamp_fusion), kind=kCustom, calls=%fused_computation.1 | custom fusion | bytes 2097168 | tf_op jit(solution)/shard_map/gather | solution.py:32
  92.6 0.0 copy-start.3
  92.6 1.0 fusion.4
  93.6 0.5 copy.11
  94.1 0.0 copy-done.3
  94.1 1.8 fusion
  95.9 1.3 copy.9
  97.2 0.0 all-reduce.3.cloned.1.call-update
  97.2 53.9 %all-reduce.5.cloned.1.call-done = f32[512,512]{1,0:T(8,128)} async-done(((f32[512,512]{1,0:T(8,128)}), f32[512,512]{1,0:T(8,128)}) %all-reduce.5.cloned.1.call-update) | async-done | bytes 1048592 | tf_op jit(solution)/shard_map/psum | solution.py:30
  151.1 2.3 %multiply_bitcast_fusion = f32[1,512,512]{2,1,0:T(8,128)} fusion(f32[512,512]{1,0:T(8,128)} %all-reduce.5.cloned.1.call-done), kind=kLoop, calls=%fused_computation.6 | loop fusion | flops 262144 | bytes 2097152 | tf_op jit(solution)/shard_map/broadcast_in_dim | solution.py:41
  153.4 51.5 %all-reduce.3.cloned.1.call-done = f32[512,512]{1,0:T(8,128)} async-done(((f32[512,512]{1,0:T(8,128)}), f32[512,512]{1,0:T(8,128)}) %all-reduce.3.cloned.1.call-update) | async-done | bytes 1048592 | tf_op jit(solution)/shard_map/psum | solution.py:40
  204.9 2.3 %copy.15 = f32[512,512]{1,0:T(8,128)} copy(f32[512,512]{1,0:T(8,128)} %all-reduce.3.cloned.1.call-done) | data formatting | bytes 2097152
  (4 shorter events, 0.0 us)
Async XLA Ops:
  7.2 1.5 copy-start
  7.2 2.1 copy-start.1
  7.2 52.6 %reduce-scatter.2.cloned.1.call-start = ((), (), s32[]{:S(2)}) async-start(), calls=%async_computation.1 | async-start | bytes 2359296 | tf_op jit(solution)/shard_map/reduce_scatter | solution.py:28
  9.3 1.5 copy-start.2
  15.7 74.6 %all-gather.2.cloned.1.call-start = ((), (), s32[]{:S(2)}) async-start(), calls=%async_computation.2 | async-start | bytes 2359296 | tf_op jit(solution)/shard_map/all_gather | solution.py:31
  59.8 91.3 %all-reduce.5.cloned.1.call-start = ((), (), s32[]{:S(2)}) async-start(), calls=%async_computation.4 | async-start | bytes 2097152 | tf_op jit(solution)/shard_map/psum | solution.py:30
  62.9 142.0 %all-reduce.3.cloned.1.call-start = ((), (), s32[]{:S(2)}) async-start(), calls=%async_computation.3 | async-start | bytes 2097152 | tf_op jit(solution)/shard_map/psum | solution.py:40
  92.6 1.5 copy-start.3
Sparse Core Ops, SparseCore 0:
  15.9 43.8 reduce-scatter.1
  62.4 27.8 all-gather.1
  94.4 56.6 all-reduce.4
  154.0 50.8 all-reduce.2
where the time goes:
time: 214 us
  waiting for transfers between devices  177 us (83%)
  between operations  14.6 us (7%)
  local copies, waits for them, and re-layouts  9.95 us (5%)
  matrix products  9.16 us (4%)
  other arithmetic  2.97 us (1%)
    psum x1, waiting for transfers between devices, local(): gram = lax.psum(local_gram, 'cols') / (RB_DEV * 128)  53.9 us
    psum x1, waiting for transfers between devices, local(): z_power = lax.psum(z_local, 'rows')  51.5 us
    reduce_scatter x1, waiting for transfers between devices, local(): lax.psum_scatter(partial_value, 'cols', scatter_dimension=0, tiled=True)  44 us
    all_gather x1, waiting for transfers between devices, local(): y_panel = lax.all_gather(y_shard, 'cols', axis=0, tiled=True)  27.4 us
  transfers between devices with their start and end apart: 4, of which 4 were waited for; matrix products, arithmetic and copies ran while one was open for 6% of the time, Pallas kernels for 0%

commit v1 on v0

v1 whole, which is shorter than its diff:
```python
import functools

import jax
import jax.numpy as jnp
from jax import lax
from jax.experimental import pallas as pl
from jax.experimental.pallas import tpu as pltpu
from jax.sharding import PartitionSpec as P

RB_DEV = 8
CB_DEV = 4
B = 128
MESH = pl.DeviceIdType.MESH
F32 = jnp.float32
BF16 = jnp.bfloat16
LAG = 1


def split2(x):
    hi = x.astype(BF16)
    return hi, (x - hi.astype(F32)).astype(BF16)


def kernel(
    n_rows, n_cols, slots,
    rows_ref, cols_ref, live_ref, tiles_ref, om_ref,
    y_out, z_out, g_out,
    codes, sib_codes, tiles_f, sib_tiles, tile_t, sib_om, om2, a_mat, a_t,
    ypart, rs_recv, ypanel, ysib, y2, yhi, ylo, zpart, zin, zcross, ztot,
    init_s, init_r, rs_s, rs_r, ag_s, ag_r, yo_s, yo_r, ys_s, ys_r,
    zc_s, zc_r, zx_r, zt_s, zt_r, zb_s, zf_s,
):
    r = lax.axis_index("rows")
    c = lax.axis_index("cols")
    core = lax.rem(c, 2)
    chip = c // 2
    other = 1 - core
    sib = chip * 2 + other
    m = n_cols // 2
    panel = RB_DEV * B
    ctx = CB_DEV * B
    rpc = panel // m
    half_rows = rpc // 2
    width = om_ref.shape[1] // 2
    chunks = width // B
    pieces = 2 * ctx // B
    mid = n_rows // 2
    lower = r < mid
    inner = jnp.where(lower, r + 1, r - 1)
    outer = jnp.where(lower, r - 1, r + 1)
    is_center = jnp.logical_or(r == mid - 1, r == mid)
    not_center = jnp.logical_not(is_center)
    has_outer = jnp.logical_and(r > 0, r < n_rows - 1)

    def remote(src, dst, ssem, rsem, dev):
        return pltpu.make_async_remote_copy(
            src_ref=src, dst_ref=dst, send_sem=ssem, recv_sem=rsem, device_id=dev, device_id_type=MESH
        )

    barrier = pltpu.get_barrier_semaphore()
    pl.semaphore_signal(barrier, inc=1, device_id=(r, sib), device_id_type=MESH)

    def greet_chip(d, _):
        pl.semaphore_signal(
            barrier, inc=1, device_id=(r, lax.rem(chip + d, m) * 2 + core), device_id_type=MESH
        )
        return 0

    lax.fori_loop(1, m, greet_chip, 0)

    def greet_row(d, _):
        row = lax.rem(r + d, n_rows)
        pl.semaphore_signal(barrier, inc=1, device_id=(row, c), device_id_type=MESH)
        pl.semaphore_signal(barrier, inc=1, device_id=(row, sib), device_id_type=MESH)
        return 0

    lax.fori_loop(1, n_rows, greet_row, 0)

    for s in range(slots):
        code = jnp.where(
            s < live_ref[0, 0], rows_ref[0, 0, s] * CB_DEV + cols_ref[0, 0, s], -1
        )
        codes[s] = jnp.full((8, B), code, jnp.int32)
        tiles_f[s] = tiles_ref[0, 0, s].astype(F32)

    pl.semaphore_wait(barrier, 1 + (m - 1) + 2 * (n_rows - 1))

    init = (
        remote(tiles_f, sib_tiles, init_s.at[0], init_r.at[0], (r, sib)),
        remote(codes, sib_codes, init_s.at[1], init_r.at[1], (r, sib)),
        remote(
            om_ref.at[:, pl.ds(pl.multiple_of(other * width, B), width)],
            sib_om, init_s.at[2], init_r.at[2], (r, sib),
        ),
    )
    for cp in init:
        cp.start()

    def place(code_ref, source, target, row0, col0, rows, cols, row_mul, col_mul):
        def line(i, _):
            for j in range(cols):
                want = i * row_mul + j * col_mul
                val = jnp.zeros((B // 8, 8, B), F32)
                for s in range(slots):
                    hit = jnp.broadcast_to((code_ref[s] == want)[None], val.shape)
                    val = jnp.where(hit, source[s].reshape(val.shape), val)
                target[pl.ds(pl.multiple_of(row0 + i * B, B), B), col0 + j * B : col0 + (j + 1) * B] = (
                    val.reshape(B, B).astype(BF16)
                )
            return 0

        lax.fori_loop(0, rows, line, 0)

    def place_om(src, col0, row0):
        for q in range(chunks):
            hi, lo = split2(src[:, pl.ds(pl.multiple_of(col0 + q * B, B), B)])
            om2[q, row0 : row0 + ctx, 0:B] = hi
            om2[q, row0 : row0 + ctx, B : 2 * B] = lo

    place(codes, tiles_f, a_mat, 0, 0, RB_DEV, CB_DEV, CB_DEV, 1)
    place_om(om_ref, core * width, 0)
    for cp in init:
        cp.wait_recv()
    place(sib_codes, sib_tiles, a_mat, 0, ctx, RB_DEV, CB_DEV, CB_DEV, 1)
    place_om(sib_om, 0, ctx)

    def chip_rows(j):
        return pl.ds(pl.multiple_of(j * rpc, 8), rpc)

    def y_rows(q, j):
        both = jnp.dot(a_mat[chip_rows(j), :], om2[q], preferred_element_type=F32)
        ypart[q, chip_rows(j), :] = both[:, :B] + both[:, B:]

    def rs_copy(q, d):
        j = lax.rem(chip + d, m)
        return remote(
            ypart.at[q, chip_rows(j), :], rs_recv.at[q, d - 1], rs_s.at[q, d - 1], rs_r.at[q, d - 1],
            (r, j * 2 + core),
        )

    def ag_copy(q, d):
        j = lax.rem(chip + d, m)
        mine = ypanel.at[q, chip_rows(chip), :]
        return remote(mine, mine, ag_s.at[q, d - 1], ag_r.at[q, d - 1], (r, j * 2 + core))

    def lanes(q):
        return pl.ds(pl.multiple_of(core * width + q * B, B), B)

    def yo_copy(q):
        return remote(
            ypanel.at[q, pl.ds(pl.multiple_of(chip * rpc + other * half_rows, 8), half_rows), :],
            y_out.at[:, lanes(q)], yo_s.at[q], yo_r.at[q], (r, sib),
        )

    def ys_copy(q):
        return remote(ypanel.at[q], ysib.at[q], ys_s.at[q], ys_r.at[q], (r, sib))

    def each_chip(fn):
        def body(d, _):
            fn(d)
            return 0

        lax.fori_loop(1, m, body, 0)

    def partial_sample(q):
        def send(d):
            y_rows(q, lax.rem(chip + d, m))
            rs_copy(q, d).start()

        each_chip(send)
        y_rows(q, chip)

    def reduce_sample(q):
        each_chip(lambda d: rs_copy(q, d).wait_recv())
        total = ypart[q, chip_rows(chip), :]
        for d in range(m - 1):
            total = total + rs_recv[q, d]
        ypanel[q, chip_rows(chip), :] = total
        each_chip(lambda d: ag_copy(q, d).start())
        yo_copy(q).start()
        y_out[:, lanes(q)] = ypanel[
            q, pl.ds(pl.multiple_of(chip * rpc + core * half_rows, 8), half_rows), :
        ]

    def gather_sample(q):
        each_chip(lambda d: ag_copy(q, d).wait_recv())
        ys_copy(q).start()
        hi, lo = split2(ypanel[q])
        y2[q, :, 0:B] = hi
        y2[q, :, B : 2 * B] = lo
        yhi[:, lanes(q)] = hi
        ylo[:, lanes(q)] = lo

    def piece_rows(i):
        k = i // 2
        start = ctx + k * B if i % 2 == 0 else k * B
        return slice(start, start + B), slice(k * B, (k + 1) * B)

    def inward(q, i, center):
        src, _ = piece_rows(i)
        dst = zcross if center else zin
        sem = zx_r if center else zc_r
        return remote(
            zpart.at[q, src, :], dst.at[q, src, :], zc_s.at[q, i], sem.at[q, i], (inner, c)
        )

    def outward(q, i):
        src, dst = piece_rows(i)
        if i % 2 == 0:
            return remote(
                ztot.at[q, dst, :], z_out.at[dst, lanes(q)], zt_s.at[q, i], zt_r.at[q, i], (outer, sib)
            )
        return remote(
            z_out.at[dst, lanes(q)], z_out.at[dst, lanes(q)], zt_s.at[q, i], zt_r.at[q, i], (outer, c)
        )

    def sideways(q, i):
        _, dst = piece_rows(i)
        return remote(
            ztot.at[q, dst, :], z_out.at[dst, lanes(q)], zb_s.at[q, i // 2], zt_r.at[q, i], (r, sib)
        )

    def other_lanes(q):
        return pl.ds(pl.multiple_of(other * width + q * B, B), B)

    def onward(q, i):
        _, dst = piece_rows(i)
        where = other_lanes(q) if i % 2 == 0 else lanes(q)
        return remote(
            z_out.at[dst, where], z_out.at[dst, where], zf_s.at[q, i], zt_r.at[q, i], (outer, c)
        )

    def finish_piece(q, i):
        src, dst = piece_rows(i)

        @pl.when(is_center)
        def _():
            inward(q, i, True).wait_recv()
            total = zpart[q, src, :] + zcross[q, src, :]
            if i % 2 == 0:
                ztot[q, dst, :] = total
                sideways(q, i).start()
            else:
                z_out[dst, lanes(q)] = total

            @pl.when(has_outer)
            def _():
                outward(q, i).start()

    def chain(q, extra):
        for i in range(pieces):
            src, _ = piece_rows(i)
            both = jnp.dot(a_t[src, :], y2[q], preferred_element_type=F32)
            zpart[q, src, :] = both[:, :B] + both[:, B:]

            @pl.when(has_outer)
            def _():
                inward(q, i, False).wait_recv()
                zpart[q, src, :] += zin[q, src, :]

            @pl.when(is_center)
            def _():
                inward(q, i, True).start()

            @pl.when(not_center)
            def _():
                inward(q, i, False).start()

            if i >= LAG:
                finish_piece(q, i - LAG)
            extra(i)
        for i in range(pieces - LAG, pieces):
            finish_piece(q, i)

    partial_sample(0)
    for s in range(slots):
        tile_t[s] = tiles_f[s].T
    place(codes, tile_t, a_t, 0, 0, CB_DEV, RB_DEV, 1, CB_DEV)
    for s in range(slots):
        tile_t[s] = sib_tiles[s].T
    place(sib_codes, tile_t, a_t, ctx, 0, CB_DEV, RB_DEV, 1, CB_DEV)

    for q in range(chunks):
        if q == 0:
            reduce_sample(0)
        gather_next = q + 1 < chunks
        if gather_next:
            partial_sample(q + 1)
        gather_sample(q)

        def extra(i):
            if gather_next:
                if i == 3:
                    reduce_sample(q + 1)
            else:
                if i == 0:
                    for t in range(chunks):
                        ys_copy(t).wait_recv()
                        hi, lo = split2(ysib[t])
                        yhi[:, other_lanes(t)] = hi
                        ylo[:, other_lanes(t)] = lo
                elif i % 2 == 1 and i // 2 < g_out.shape[1] // B:
                    gram_rows(i // 2)

        def gram_rows(j):
            dims = (((0,), (0,)), ((), ()))
            cols = slice(j * B, (j + 1) * B)
            hi_j, lo_j = yhi[:, cols], ylo[:, cols]
            g = lax.dot_general(hi_j, yhi[...], dims, preferred_element_type=F32)
            g += lax.dot_general(hi_j, ylo[...], dims, preferred_element_type=F32)
            g += lax.dot_general(lo_j, yhi[...], dims, preferred_element_type=F32)
            g_out[0, cols, :] = g * (1.0 / (RB_DEV * B))

        chain(q, extra)

    for q in range(chunks):
        for i in range(pieces):
            if i % 2 == 0:
                outward(q, i).wait_recv()
            else:

                @pl.when(not_center)
                def _():
                    outward(q, i).wait_recv()

            if n_rows > 4:

                @pl.when(jnp.logical_and(has_outer, not_center))
                def _():
                    onward(q, i).start()

    for cp in init:
        cp.wait_send()
    for q in range(chunks):
        each_chip(lambda d: rs_copy(q, d).wait_send())
        each_chip(lambda d: ag_copy(q, d).wait_send())
        yo_copy(q).wait()
        ys_copy(q).wait_send()
        for i in range(pieces):
            inward(q, i, True).wait_send()

            @pl.when(is_center)
            def _():
                if i % 2 == 0:
                    sideways(q, i).wait_send()

                @pl.when(has_outer)
                def _():
                    outward(q, i).wait_send()

            if n_rows > 4:

                @pl.when(jnp.logical_and(has_outer, not_center))
                def _():
                    onward(q, i).wait_send()


def solution(mesh):
    n_rows, n_cols = mesh.shape["rows"], mesh.shape["cols"]

    def local(tile_values, tile_rows, tile_cols, live_counts, test_block):
        slots = tile_values.shape[2]
        test_cols = test_block.shape[1]
        m = n_cols // 2
        panel, ctx = RB_DEV * B, CB_DEV * B
        width = test_cols // 2
        chunks = width // B
        pieces = 2 * ctx // B
        vmem = pl.BlockSpec(memory_space=pltpu.VMEM)
        smem = pl.BlockSpec(memory_space=pltpu.SMEM)
        dma = pltpu.SemaphoreType.DMA
        return pl.pallas_call(
            functools.partial(kernel, n_rows, n_cols, slots),
            out_shape=(
                jax.ShapeDtypeStruct((panel // n_cols, test_cols), F32),
                jax.ShapeDtypeStruct((ctx, test_cols), F32),
                jax.ShapeDtypeStruct((1, test_cols, test_cols), F32),
            ),
            in_specs=[smem, smem, smem, vmem, vmem],
            out_specs=(vmem, vmem, vmem),
            scratch_shapes=[
                pltpu.VMEM((slots, 8, B), jnp.int32),
                pltpu.VMEM((slots, 8, B), jnp.int32),
                pltpu.VMEM((slots, B, B), F32),
                pltpu.VMEM((slots, B, B), F32),
                pltpu.VMEM((slots, B, B), F32),
                pltpu.VMEM((ctx, width), F32),
                pltpu.VMEM((chunks, 2 * ctx, 2 * B), BF16),
                pltpu.VMEM((panel, 2 * ctx), BF16),
                pltpu.VMEM((2 * ctx, panel), BF16),
                pltpu.VMEM((chunks, panel, B), F32),
                pltpu.VMEM((chunks, m - 1, panel // m, B), F32),
                pltpu.VMEM((chunks, panel, B), F32),
                pltpu.VMEM((chunks, panel, B), F32),
                pltpu.VMEM((chunks, panel, 2 * B), BF16),
                pltpu.VMEM((panel, test_cols), BF16),
                pltpu.VMEM((panel, test_cols), BF16),
                pltpu.VMEM((chunks, 2 * ctx, B), F32),
                pltpu.VMEM((chunks, 2 * ctx, B), F32),
                pltpu.VMEM((chunks, 2 * ctx, B), F32),
                pltpu.VMEM((chunks, ctx, B), F32),
                dma((3,)), dma((3,)),
                dma((chunks, m - 1)), dma((chunks, m - 1)),
                dma((chunks, m - 1)), dma((chunks, m - 1)),
                dma((chunks,)), dma((chunks,)),
                dma((chunks,)), dma((chunks,)),
                dma((chunks, pieces)), dma((chunks, pieces)), dma((chunks, pieces)),
                dma((chunks, pieces)), dma((chunks, pieces)),
                dma((chunks, pieces)), dma((chunks, pieces)),
            ],
            compiler_params=pltpu.CompilerParams(
                collective_id=0, has_side_effects=True, vmem_limit_bytes=48 * 1024 * 1024
            ),
            cost_estimate=pl.CostEstimate(flops=4_000_000_000, bytes_accessed=4_000_000, transcendentals=0),
        )(tile_rows, tile_cols, live_counts, tile_values, test_block)

    return jax.shard_map(
        local,
        mesh=mesh,
        in_specs=(
            P("rows", "cols", None, None, None),
            P("rows", "cols", None),
            P("rows", "cols", None),
            P("rows", "cols"),
            P("cols", None),
        ),
        out_specs=(P(("rows", "cols"), None), P("cols", None), P("rows", None, None)),
        check_vma=False,
    )
```

time: 214 us -> 74.8 us (0.35)
  waiting for transfers between devices: 177 us -> 0 us
  Pallas kernels: 0 us -> 68.5 us
  between operations: 14.6 us -> 1.35 us
  matrix products: 9.16 us -> 0 us
  local copies, waits for them, and re-layouts: 9.95 us -> 4.77 us
  other arithmetic: 2.97 us -> 0 us
    psum x2 -> x0, waiting for transfers between devices: 105 us -> none  [the longest x1 53.9 us: local(): gram = lax.psum(local_gram, 'cols') / (RB_DEV * 128)]
    pallas_call x0 -> x1, Pallas kernels: none -> 68.5 us  [local(): pl.pallas_call(functools.partial(kernel, n_rows, n_cols, slots), out_shap...]
    reduce_scatter x1 -> x0, waiting for transfers between devices: 44 us -> none  [local(): lax.psum_scatter(partial_value, 'cols', scatter_dimension=0, tiled=True)]
    all_gather x1 -> x0, waiting for transfers between devices: 27.4 us -> none  [local(): y_panel = lax.all_gather(y_shard, 'cols', axis=0, tiled=True)]
    dot_general x5 -> x0, matrix products: 9.16 us -> none  [the longest x1 3.03 us: local(): jnp.dot(y_shard.T, y_shard, precision=high, preferred_element_type=jnp.fl...]
    dot_general x4 -> x0, local copies, waits for them, and re-layouts: 4.84 us -> none  [the longest x1 2.57 us: local(): jnp.einsum('sr,sak->rak', row_onehot, products, precision=high)]
    gather x2 -> x0, local copies, waits for them, and re-layouts: 2.82 us -> none  [the longest x1 2.2 us: local(): y_tiles = y_panel.reshape(RB_DEV, 128, test_cols)[rows_local]]
    unnamed x9 -> x11, local copies, waits for them, and re-layouts: 2.29 us -> 4.77 us
  transfers between devices with their start and end apart: 4 -> 0, of which waited for: 4 -> 0; matrix products, arithmetic and copies ran while one was open for 6% -> 0% of each run, Pallas kernels for 0% -> 0%
where the time goes in v1:
time: 74.8 us; the launch traced here: 74.7 us
  Pallas kernels  68.5 us (92%)
  local copies, waits for them, and re-layouts  4.77 us (6%)
  between operations  1.35 us (2%)
    pallas_call x1, Pallas kernels, local(): pl.pallas_call(functools.partial(kernel, n_rows, n_cols, slots), out_shap...  68.5 us
    unnamed x11, local copies, waits for them, and re-layouts  4.77 us

profile of v1, /device:TPU:0, one launch (start us, length us, event | category | flops | bytes accessed | tf_op | source)
XLA Modules:
  0.0 74.7 jit_solution(13591376278164075321)
XLA Ops:
  0.6 0.0 copy-start.3
  0.6 0.0 copy-start.2
  1.3 0.0 copy-done.3
  1.3 0.0 copy-done.2
  1.3 0.0 copy-start
  1.3 1.2 %copy-done = f32[512,512]{1,0:T(8,128)S(1)} copy-done((f32[512,512]{1,0:T(8,128)S(1)}, f32[512,512]{1,0:T(8,128)}, u32[]{:S(2)}) %copy-start) | copy-done | bytes 1048600
  2.6 0.0 copy-start.1
  2.6 0.9 %copy-done.1 = bf16[1,1,4,128,128]{4,3,2,1,0:T(8,128)(2,1)S(1)} copy-done((bf16[1,1,4,128,128]{4,3,2,1,0:T(8,128)(2,1)S(1)}, bf16[1,1,4,128,128]{4,3,2,1,0:T(8,128)(2,1)}, u32[]{:S(2)}) %copy-start.1) | copy-done | bytes 131096
  3.5 68.5 %shard_map.76 = (f32[128,512]{1,0:T(8,128)S(1)}, f32[512,512]{1,0:T(8,128)S(1)}, f32[1,512,512]{2,1,0:T(8,128)S(1)}) custom-call(s32[1,1,4]{2,1,0:T(1,128)S(1)} %copy-done.2, s32[1,1,4]{2,1,0:T(1,128)S(1)} %copy-done.3, s32[1,1]{1,0:T(1,128)S(6)} %copy.11.live_ref, bf16[1,1,4,128,128]{4,3,2,1,0:T(8,128)(2,1)S(1)} %copy-done.1, f32[512,512]{1,0:T(8,128)S(1)} %copy-done), custom_call_target="tpu_custom_call" | custom-call | flops 4000000000 | bytes 4000000 | tf_op jit(solution)/shard_map/pallas_call | solution.py:372
  72.0 0.7 copy.12
  72.7 1.0 %copy.13 = f32[512,512]{1,0:T(8,128)} copy(f32[512,512]{1,0:T(8,128)S(1)} %get-tuple-element.7) | data formatting | bytes 2097152
  73.7 1.0 %copy.14 = f32[1,512,512]{2,1,0:T(8,128)} copy(f32[1,512,512]{2,1,0:T(8,128)S(1)} %get-tuple-element.8) | data formatting | bytes 2097152
Async XLA Ops:
  0.6 0.7 copy-start.3
  0.6 0.7 copy-start.2
  1.3 1.2 %copy-start = (f32[512,512]{1,0:T(8,128)S(1)}, f32[512,512]{1,0:T(8,128)}, u32[]{:S(2)}) copy-start(f32[512,512]{1,0:T(8,128)} %om_ref.1) | copy-start | bytes 3145732
  2.6 0.9 %copy-start.1 = (bf16[1,1,4,128,128]{4,3,2,1,0:T(8,128)(2,1)S(1)}, bf16[1,1,4,128,128]{4,3,2,1,0:T(8,128)(2,1)}, u32[]{:S(2)}) copy-start(bf16[1,1,4,128,128]{4,3,2,1,0:T(8,128)(2,1)} %tiles_ref.1) | copy-start | bytes 393220

commit v2 on v1

--- a/solution.py
+++ b/solution.py
@@ -28,7 +28,7 @@
     codes, sib_codes, tiles_f, sib_tiles, tile_t, sib_om, om2, a_mat, a_t,
     ypart, rs_recv, ypanel, ysib, y2, yhi, ylo, zpart, zin, zcross, ztot,
     init_s, init_r, rs_s, rs_r, ag_s, ag_r, yo_s, yo_r, ys_s, ys_r,
-    zc_s, zc_r, zx_r, zt_s, zt_r, zb_s, zf_s,
+    zc_s, zc_r, zx_r, zt_s, zt_r, zb_s, zf_s, tiles_in, om_in, load_s,
 ):
     r = lax.axis_index("rows")
     c = lax.axis_index("cols")
@@ -45,6 +45,7 @@
     chunks = width // B
     pieces = 2 * ctx // B
     mid = n_rows // 2
+    gram_steps = (1, 3, 5, 6)
     lower = r < mid
     inner = jnp.where(lower, r + 1, r - 1)
     outer = jnp.where(lower, r - 1, r + 1)
@@ -57,6 +58,13 @@
             src_ref=src, dst_ref=dst, send_sem=ssem, recv_sem=rsem, device_id=dev, device_id_type=MESH
         )
 
+    load_tiles = pltpu.make_async_copy(tiles_ref.at[0, 0], tiles_in, load_s.at[0])
+    load_om = pltpu.make_async_copy(
+        om_ref.at[:, pl.ds(pl.multiple_of(core * width, B), width)], om_in, load_s.at[1]
+    )
+    load_tiles.start()
+    load_om.start()
+
     barrier = pltpu.get_barrier_semaphore()
     pl.semaphore_signal(barrier, inc=1, device_id=(r, sib), device_id_type=MESH)
 
@@ -76,12 +84,13 @@
 
     lax.fori_loop(1, n_rows, greet_row, 0)
 
+    load_tiles.wait()
     for s in range(slots):
         code = jnp.where(
             s < live_ref[0, 0], rows_ref[0, 0, s] * CB_DEV + cols_ref[0, 0, s], -1
         )
         codes[s] = jnp.full((8, B), code, jnp.int32)
-        tiles_f[s] = tiles_ref[0, 0, s].astype(F32)
+        tiles_f[s] = tiles_in[s].astype(F32)
 
     pl.semaphore_wait(barrier, 1 + (m - 1) + 2 * (n_rows - 1))
 
@@ -111,18 +120,19 @@
 
         lax.fori_loop(0, rows, line, 0)
 
-    def place_om(src, col0, row0):
+    def place_om(src, row0):
         for q in range(chunks):
-            hi, lo = split2(src[:, pl.ds(pl.multiple_of(col0 + q * B, B), B)])
+            hi, lo = split2(src[:, q * B : (q + 1) * B])
             om2[q, row0 : row0 + ctx, 0:B] = hi
             om2[q, row0 : row0 + ctx, B : 2 * B] = lo
 
     place(codes, tiles_f, a_mat, 0, 0, RB_DEV, CB_DEV, CB_DEV, 1)
-    place_om(om_ref, core * width, 0)
+    load_om.wait()
+    place_om(om_in, 0)
     for cp in init:
         cp.wait_recv()
     place(sib_codes, sib_tiles, a_mat, 0, ctx, RB_DEV, CB_DEV, CB_DEV, 1)
-    place_om(sib_om, 0, ctx)
+    place_om(sib_om, ctx)
 
     def chip_rows(j):
         return pl.ds(pl.multiple_of(j * rpc, 8), rpc)
@@ -168,6 +178,10 @@
             rs_copy(q, d).start()
 
         each_chip(send)
+        y_rows(q, chip)
+
+    def prepare_sample(q):
+        each_chip(lambda d: y_rows(q, lax.rem(chip + d, m)))
         y_rows(q, chip)
 
     def reduce_sample(q):
@@ -182,8 +196,10 @@
             q, pl.ds(pl.multiple_of(chip * rpc + core * half_rows, 8), half_rows), :
         ]
 
-    def gather_sample(q):
+    def gather_sample(q, following):
         each_chip(lambda d: ag_copy(q, d).wait_recv())
+        if following is not None:
+            each_chip(lambda d: rs_copy(following, d).start())
         ys_copy(q).start()
         hi, lo = split2(ypanel[q])
         y2[q, :, 0:B] = hi
@@ -285,22 +301,35 @@
             reduce_sample(0)
         gather_next = q + 1 < chunks
         if gather_next:
-            partial_sample(q + 1)
-        gather_sample(q)
+            prepare_sample(q + 1)
+        gather_sample(q, q + 1 if gather_next else None)
+
+        def collect_gram():
+            for t in range(chunks):
+                ys_copy(t).wait_recv()
+                hi, lo = split2(ysib[t])
+                yhi[:, other_lanes(t)] = hi
+                ylo[:, other_lanes(t)] = lo
 
         def extra(i):
             if gather_next:
                 if i == 3:
-                    reduce_sample(q + 1)
-            else:
-                if i == 0:
-                    for t in range(chunks):
-                        ys_copy(t).wait_recv()
-                        hi, lo = split2(ysib[t])
-                        yhi[:, other_lanes(t)] = hi
-                        ylo[:, other_lanes(t)] = lo
-                elif i % 2 == 1 and i // 2 < g_out.shape[1] // B:
-                    gram_rows(i // 2)
+                    pl.when(is_center)(lambda: reduce_sample(q + 1))
+                if i == pieces - 1:
+                    pl.when(not_center)(lambda: reduce_sample(q + 1))
+                return
+            blocks = g_out.shape[1] // B
+            if i == 0:
+                pl.when(is_center)(collect_gram)
+            if i in gram_steps[:blocks]:
+                pl.when(is_center)(lambda: gram_rows(gram_steps.index(i)))
+            if i == pieces - 1:
+
+                @pl.when(not_center)
+                def _():
+                    collect_gram()
+                    for j in range(blocks):
+                        gram_rows(j)
 
         def gram_rows(j):
             dims = (((0,), (0,)), ((), ()))
@@ -368,6 +397,7 @@
         pieces = 2 * ctx // B
         vmem = pl.BlockSpec(memory_space=pltpu.VMEM)
         smem = pl.BlockSpec(memory_space=pltpu.SMEM)
+        hbm = pl.BlockSpec(memory_space=pl.ANY)
         dma = pltpu.SemaphoreType.DMA
         return pl.pallas_call(
             functools.partial(kernel, n_rows, n_cols, slots),
@@ -376,7 +406,7 @@
                 jax.ShapeDtypeStruct((ctx, test_cols), F32),
                 jax.ShapeDtypeStruct((1, test_cols, test_cols), F32),
             ),
-            in_specs=[smem, smem, smem, vmem, vmem],
+            in_specs=[smem, smem, smem, hbm, hbm],
             out_specs=(vmem, vmem, vmem),
             scratch_shapes=[
                 pltpu.VMEM((slots, 8, B), jnp.int32),
@@ -407,6 +437,9 @@
                 dma((chunks, pieces)), dma((chunks, pieces)), dma((chunks, pieces)),
                 dma((chunks, pieces)), dma((chunks, pieces)),
                 dma((chunks, pieces)), dma((chunks, pieces)),
+                pltpu.VMEM((slots, B, B), BF16),
+                pltpu.VMEM((ctx, width), F32),
+                dma((2,)),
             ],
             compiler_params=pltpu.CompilerParams(
                 collective_id=0, has_side_effects=True, vmem_limit_bytes=48 * 1024 * 1024

time: 74.8 us -> 74.3 us (level)
  no operation moved by 1% of the time
where the time goes in v2:
time: 74.3 us; the launch traced here: 74.1 us
  Pallas kernels  68 us (92%)
  local copies, waits for them, and re-layouts  4.77 us (6%)
  between operations  1.35 us (2%)
    pallas_call x1, Pallas kernels, local(): pl.pallas_call(functools.partial(kernel, n_rows, n_cols, slots), out_shap...  68 us
    unnamed x11, local copies, waits for them, and re-layouts  4.77 us

profile of v2, /device:TPU:0, one launch (start us, length us, event | category | flops | bytes accessed | tf_op | source)
XLA Modules:
  0.0 74.1 jit_solution(2376812404113535056)
XLA Ops:
  0.6 0.0 copy-start.3
  0.6 0.0 copy-start.2
  1.3 0.0 copy-done.3
  1.3 0.0 copy-done.2
  1.3 0.0 copy-start
  1.3 1.2 %copy-done = f32[512,512]{1,0:T(8,128)S(1)} copy-done((f32[512,512]{1,0:T(8,128)S(1)}, f32[512,512]{1,0:T(8,128)}, u32[]{:S(2)}) %copy-start) | copy-done | bytes 1048600
  2.6 0.0 copy-start.1
  2.6 0.9 %copy-done.1 = bf16[1,1,4,128,128]{4,3,2,1,0:T(8,128)(2,1)S(1)} copy-done((bf16[1,1,4,128,128]{4,3,2,1,0:T(8,128)(2,1)S(1)}, bf16[1,1,4,128,128]{4,3,2,1,0:T(8,128)(2,1)}, u32[]{:S(2)}) %copy-start.1) | copy-done | bytes 131096
  3.5 68.0 %shard_map.76 = (f32[128,512]{1,0:T(8,128)S(1)}, f32[512,512]{1,0:T(8,128)S(1)}, f32[1,512,512]{2,1,0:T(8,128)S(1)}) custom-call(s32[1,1,4]{2,1,0:T(1,128)S(1)} %copy-done.2, s32[1,1,4]{2,1,0:T(1,128)S(1)} %copy-done.3, s32[1,1]{1,0:T(1,128)S(6)} %copy.11.live_ref, bf16[1,1,4,128,128]{4,3,2,1,0:T(8,128)(2,1)S(1)} %copy-done.1, f32[512,512]{1,0:T(8,128)S(1)} %copy-done), custom_call_target="tpu_custom_call" | custom-call | flops 4000000000 | bytes 4000000 | tf_op jit(solution)/shard_map/pallas_call | solution.py:402
  71.5 0.7 copy.12
  72.2 1.0 %copy.13 = f32[512,512]{1,0:T(8,128)} copy(f32[512,512]{1,0:T(8,128)S(1)} %get-tuple-element.7) | data formatting | bytes 2097152
  73.2 1.0 %copy.14 = f32[1,512,512]{2,1,0:T(8,128)} copy(f32[1,512,512]{2,1,0:T(8,128)S(1)} %get-tuple-element.8) | data formatting | bytes 2097152
Async XLA Ops:
  0.6 0.7 copy-start.3
  0.6 0.7 copy-start.2
  1.3 1.2 %copy-start = (f32[512,512]{1,0:T(8,128)S(1)}, f32[512,512]{1,0:T(8,128)}, u32[]{:S(2)}) copy-start(f32[512,512]{1,0:T(8,128)} %om_ref.1) | copy-start | bytes 3145732
  2.6 0.9 %copy-start.1 = (bf16[1,1,4,128,128]{4,3,2,1,0:T(8,128)(2,1)S(1)}, bf16[1,1,4,128,128]{4,3,2,1,0:T(8,128)(2,1)}, u32[]{:S(2)}) copy-start(bf16[1,1,4,128,128]{4,3,2,1,0:T(8,128)(2,1)} %tiles_ref.1) | copy-start | bytes 393220

commit v3 on v0

v3 whole, which is shorter than its diff:
```python
import functools

import jax
import jax.numpy as jnp
from jax import lax
from jax.experimental import pallas as pl
from jax.experimental.pallas import tpu as pltpu
from jax.sharding import PartitionSpec as P

RB_DEV = 8
CB_DEV = 4
B = 128
MESH = pl.DeviceIdType.MESH
F32 = jnp.float32
BF16 = jnp.bfloat16
LAG = 1


def split2(x):
    hi = x.astype(BF16)
    return hi, (x - hi.astype(F32)).astype(BF16)


def kernel(
    n_rows, n_cols, slots,
    rows_ref, cols_ref, live_ref, tiles_ref, om_ref,
    y_out, z_out, g_out,
    codes, sib_codes, tiles_in, tiles_f, sib_tiles, tile_t, om_in, sib_om, om2, a_mat, a_t,
    ypart, rs_recv, ypanel, y2, yhi, ylo, zpart, zin, zcross,
    load_s, init_s, init_r, om_s, om_r, rs_s, rs_r, ag_s, ag_r, sb_s, sb_r,
    zc_s, zc_r, zx_r, zt_s, zt_r, zf_s,
):
    r = lax.axis_index("rows")
    c = lax.axis_index("cols")
    core = lax.rem(c, 2)
    chip = c // 2
    other = 1 - core
    sib = chip * 2 + other
    m = n_cols // 2
    panel = RB_DEV * B
    ctx = CB_DEV * B
    share = panel // n_cols
    compact = share == B
    chunks = om_ref.shape[1] // B
    pieces = ctx // B
    mid = n_rows // 2
    lower = r < mid
    inner = jnp.where(lower, r + 1, r - 1)
    outer = jnp.where(lower, r - 1, r + 1)
    is_center = jnp.logical_or(r == mid - 1, r == mid)
    not_center = jnp.logical_not(is_center)
    has_outer = jnp.logical_and(r > 0, r < n_rows - 1)

    def remote(src, dst, ssem, rsem, dev):
        return pltpu.make_async_remote_copy(
            src_ref=src, dst_ref=dst, send_sem=ssem, recv_sem=rsem, device_id=dev, device_id_type=MESH
        )

    def each_chip(fn):
        def body(d, _):
            fn(d)
            return 0

        lax.fori_loop(1, m, body, 0)

    def lanes(q):
        return slice(q * B, (q + 1) * B)

    load_tiles = pltpu.make_async_copy(tiles_ref.at[0, 0], tiles_in, load_s.at[0])
    load_om = [
        pltpu.make_async_copy(om_ref.at[:, lanes(q)], om_in.at[q], load_s.at[1 + q]) for q in range(chunks)
    ]
    load_tiles.start()
    for cp in load_om:
        cp.start()

    barrier = pltpu.get_barrier_semaphore()
    pl.semaphore_signal(barrier, inc=1, device_id=(r, sib), device_id_type=MESH)

    def greet_chip(d):
        pl.semaphore_signal(
            barrier, inc=1, device_id=(r, lax.rem(chip + d, m) * 2 + core), device_id_type=MESH
        )

    each_chip(greet_chip)

    def greet_row(d, _):
        pl.semaphore_signal(barrier, inc=1, device_id=(lax.rem(r + d, n_rows), c), device_id_type=MESH)
        return 0

    lax.fori_loop(1, n_rows, greet_row, 0)

    load_tiles.wait()
    for s in range(slots):
        code = jnp.where(
            s < live_ref[0, 0], rows_ref[0, 0, s] * CB_DEV + cols_ref[0, 0, s], -1
        )
        codes[s] = jnp.full((8, B), code, jnp.int32)
        tiles_f[s] = tiles_in[s].astype(F32)

    pl.semaphore_wait(barrier, 1 + (m - 1) + (n_rows - 1))

    init = (
        remote(tiles_f, sib_tiles, init_s.at[0], init_r.at[0], (r, sib)),
        remote(codes, sib_codes, init_s.at[1], init_r.at[1], (r, sib)),
    )
    om_swap = [
        remote(om_ref.at[:, lanes(q)], sib_om.at[q], om_s.at[q], om_r.at[q], (r, sib)) for q in range(chunks)
    ]
    for cp in (*init, *om_swap):
        cp.start()

    def place(code_ref, source, target, col0, rows, cols, want):
        def line(i, _):
            for j in range(cols):
                code = want(i, j)
                val = jnp.zeros((B // 8, 8, B), F32)
                for s in range(slots):
                    hit = jnp.broadcast_to((code_ref[s] == code)[None], val.shape)
                    val = jnp.where(hit, source[s].reshape(val.shape), val)
                target[pl.ds(pl.multiple_of(i * B, B), B), col0 + j * B : col0 + (j + 1) * B] = (
                    val.reshape(B, B).astype(BF16)
                )
            return 0

        lax.fori_loop(0, rows, line, 0)

    def place_om(q, src, row0):
        hi, lo = split2(src[q])
        om2[q, row0 : row0 + ctx, 0:B] = hi
        om2[q, row0 : row0 + ctx, B : 2 * B] = lo

    if compact:
        a_rows, row_code = m, lambda i, j: (2 * i + core) * CB_DEV + j
    else:
        a_rows, row_code = RB_DEV, lambda i, j: i * CB_DEV + j

    def part_rows(j):
        start = j * share if compact else (2 * j + core) * share
        return pl.ds(pl.multiple_of(start, 8), share)

    def panel_rows(j, parity):
        return pl.ds(pl.multiple_of((2 * j + parity) * share, 8), share)

    def rs_copy(q, d):
        j = lax.rem(chip + d, m)
        return remote(
            ypart.at[q, part_rows(j), :], rs_recv.at[q, d - 1], rs_s.at[q, d - 1], rs_r.at[q, d - 1],
            (r, j * 2 + core),
        )

    def ag_copy(q, d):
        j = lax.rem(chip + d, m)
        mine = ypanel.at[q, panel_rows(chip, core), :]
        return remote(mine, mine, ag_s.at[q, d - 1], ag_r.at[q, d - 1], (r, j * 2 + core))

    def sb_copy(q, d):
        block = ypanel.at[q, panel_rows(lax.rem(chip + m - d, m), core), :]
        return remote(block, block, sb_s.at[q, d], sb_r.at[q, d], (r, sib))

    def partial_sample(q):
        load_om[q].wait()
        place_om(q, om_in, 0)
        om_swap[q].wait_recv()
        place_om(q, sib_om, ctx)
        step = 2 * B
        for k in range(a_rows * B // step):
            rows = slice(k * step, (k + 1) * step)
            both = jnp.dot(a_mat[rows, :], om2[q], preferred_element_type=F32)
            ypart[q, rows, :] = both[:, :B] + both[:, B:]

    def send_sample(q):
        each_chip(lambda d: rs_copy(q, d).start())

    def reduce_sample(q):
        each_chip(lambda d: rs_copy(q, d).wait_recv())
        total = ypart[q, part_rows(chip), :]
        for d in range(m - 1):
            total = total + rs_recv[q, d]
        ypanel[q, panel_rows(chip, core), :] = total
        each_chip(lambda d: ag_copy(q, d).start())
        sb_copy(q, 0).start()
        y_out[:, lanes(q)] = total

    def swap_sample(q):
        def step(d):
            ag_copy(q, d).wait_recv()
            sb_copy(q, d).start()

        each_chip(step)

    def finish_sample(q):
        sb_copy(q, 0).wait_recv()
        each_chip(lambda d: sb_copy(q, d).wait_recv())
        hi, lo = split2(ypanel[q])
        y2[q, :, 0:B] = hi
        y2[q, :, B : 2 * B] = lo
        yhi[:, lanes(q)] = hi
        ylo[:, lanes(q)] = lo

    def gram_rows(q):
        dims = (((0,), (0,)), ((), ()))
        upto = slice(0, (q + 1) * B)
        hi_q, lo_q = yhi[:, lanes(q)], ylo[:, lanes(q)]
        g = lax.dot_general(hi_q, yhi[:, upto], dims, preferred_element_type=F32)
        g += lax.dot_general(hi_q, ylo[:, upto], dims, preferred_element_type=F32)
        g += lax.dot_general(lo_q, yhi[:, upto], dims, preferred_element_type=F32)
        g = g * (1.0 / (RB_DEV * B))
        g_out[0, lanes(q), upto] = g
        for j in range(q):
            g_out[0, lanes(j), lanes(q)] = g[:, lanes(j)].T

    def inward(q, i, center):
        dst = zcross if center else zin
        sem = zx_r if center else zc_r
        return remote(
            zpart.at[q, lanes(i), :], dst.at[q, lanes(i), :], zc_s.at[q, i], sem.at[q, i], (inner, c)
        )

    def outward(q, i):
        piece = z_out.at[lanes(i), lanes(q)]
        return remote(piece, piece, zt_s.at[q, i], zt_r.at[q, i], (outer, c))

    def onward(q, i):
        piece = z_out.at[lanes(i), lanes(q)]
        return remote(piece, piece, zf_s.at[q, i], zt_r.at[q, i], (outer, c))

    def finish_piece(q, i):
        @pl.when(is_center)
        def _():
            inward(q, i, True).wait_recv()
            z_out[lanes(i), lanes(q)] = zpart[q, lanes(i), :] + zcross[q, lanes(i), :]

            @pl.when(has_outer)
            def _():
                outward(q, i).start()

    def chain_piece(q, i):
        both = jnp.dot(a_t[lanes(i), :], y2[q], preferred_element_type=F32)
        zpart[q, lanes(i), :] = both[:, :B] + both[:, B:]

        @pl.when(has_outer)
        def _():
            inward(q, i, False).wait_recv()
            zpart[q, lanes(i), :] += zin[q, lanes(i), :]

        @pl.when(is_center)
        def _():
            inward(q, i, True).start()

        @pl.when(not_center)
        def _():
            inward(q, i, False).start()

    place(codes, tiles_f, a_mat, 0, a_rows, CB_DEV, row_code)
    for cp in init:
        cp.wait_recv()
    place(sib_codes, sib_tiles, a_mat, ctx, a_rows, CB_DEV, row_code)
    partial_sample(0)
    send_sample(0)
    for s in range(slots):
        tile_t[s] = tiles_f[s].T
    place(codes, tile_t, a_t, 0, CB_DEV, RB_DEV, lambda i, j: j * CB_DEV + i)
    if chunks > 1:
        partial_sample(1)
    reduce_sample(0)
    if chunks > 1:
        send_sample(1)
    if chunks > 2:
        partial_sample(2)
    swap_sample(0)
    finish_sample(0)

    late = []
    for q in range(chunks):
        for i in range(pieces):
            chain_piece(q, i)
            late.append((q, i))
            if len(late) > LAG:
                finish_piece(*late.pop(0))
            if i == 0 and q + 1 < chunks:
                reduce_sample(q + 1)
                if q + 2 < chunks:
                    send_sample(q + 2)
            if i == 1:
                gram_rows(q)
                if q + 3 < chunks:
                    partial_sample(q + 3)
            if i == 2 and q + 1 < chunks:
                swap_sample(q + 1)
        if q + 1 < chunks:
            finish_sample(q + 1)
    for item in late:
        finish_piece(*item)

    for q in range(chunks):
        for i in range(pieces):

            @pl.when(not_center)
            def _():
                outward(q, i).wait_recv()

            if n_rows > 4:

                @pl.when(jnp.logical_and(has_outer, not_center))
                def _():
                    onward(q, i).start()

    for cp in (*init, *om_swap):
        cp.wait_send()
    for q in range(chunks):
        each_chip(lambda d: rs_copy(q, d).wait_send())
        each_chip(lambda d: ag_copy(q, d).wait_send())
        sb_copy(q, 0).wait_send()
        each_chip(lambda d: sb_copy(q, d).wait_send())
        for i in range(pieces):
            inward(q, i, True).wait_send()

            @pl.when(jnp.logical_and(is_center, has_outer))
            def _():
                outward(q, i).wait_send()

            if n_rows > 4:

                @pl.when(jnp.logical_and(has_outer, not_center))
                def _():
                    onward(q, i).wait_send()


def solution(mesh):
    n_rows, n_cols = mesh.shape["rows"], mesh.shape["cols"]

    def local(tile_values, tile_rows, tile_cols, live_counts, test_block):
        slots = tile_values.shape[2]
        test_cols = test_block.shape[1]
        m = n_cols // 2
        panel, ctx = RB_DEV * B, CB_DEV * B
        chunks = test_cols // B
        pieces = ctx // B
        share = panel // n_cols
        used = m * B if share == B else panel
        vmem = pl.BlockSpec(memory_space=pltpu.VMEM)
        smem = pl.BlockSpec(memory_space=pltpu.SMEM)
        hbm = pl.BlockSpec(memory_space=pltpu.HBM)
        dma = pltpu.SemaphoreType.DMA
        return pl.pallas_call(
            functools.partial(kernel, n_rows, n_cols, slots),
            out_shape=(
                jax.ShapeDtypeStruct((panel // n_cols, test_cols), F32),
                jax.ShapeDtypeStruct((ctx, test_cols), F32),
                jax.ShapeDtypeStruct((1, test_cols, test_cols), F32),
            ),
            in_specs=[smem, smem, smem, hbm, hbm],
            out_specs=(vmem, vmem, vmem),
            scratch_shapes=[
                pltpu.VMEM((slots, 8, B), jnp.int32),
                pltpu.VMEM((slots, 8, B), jnp.int32),
                pltpu.VMEM((slots, B, B), BF16),
                pltpu.VMEM((slots, B, B), F32),
                pltpu.VMEM((slots, B, B), F32),
                pltpu.VMEM((slots, B, B), F32),
                pltpu.VMEM((chunks, ctx, B), F32),
                pltpu.VMEM((chunks, ctx, B), F32),
                pltpu.VMEM((chunks, 2 * ctx, 2 * B), BF16),
                pltpu.VMEM((used, 2 * ctx), BF16),
                pltpu.VMEM((ctx, panel), BF16),
                pltpu.VMEM((chunks, used, B), F32),
                pltpu.VMEM((chunks, m - 1, share, B), F32),
                pltpu.VMEM((chunks, panel, B), F32),
                pltpu.VMEM((chunks, panel, 2 * B), BF16),
                pltpu.VMEM((panel, test_cols), BF16),
                pltpu.VMEM((panel, test_cols), BF16),
                pltpu.VMEM((chunks, ctx, B), F32),
                pltpu.VMEM((chunks, ctx, B), F32),
                pltpu.VMEM((chunks, ctx, B), F32),
                dma((1 + chunks,)),
                dma((2,)), dma((2,)),
                dma((chunks,)), dma((chunks,)),
                dma((chunks, m - 1)), dma((chunks, m - 1)),
                dma((chunks, m - 1)), dma((chunks, m - 1)),
                dma((chunks, m)), dma((chunks, m)),
                dma((chunks, pieces)), dma((chunks, pieces)), dma((chunks, pieces)),
                dma((chunks, pieces)), dma((chunks, pieces)), dma((chunks, pieces)),
            ],
            compiler_params=pltpu.CompilerParams(
                collective_id=0, has_side_effects=True, vmem_limit_bytes=60 * 1024 * 1024
            ),
            cost_estimate=pl.CostEstimate(flops=4_000_000_000, bytes_accessed=4_000_000, transcendentals=0),
        )(tile_rows, tile_cols, live_counts, tile_values, test_block)

    return jax.shard_map(
        local,
        mesh=mesh,
        in_specs=(
            P("rows", "cols", None, None, None),
            P("rows", "cols", None),
            P("rows", "cols", None),
            P("rows", "cols"),
            P("cols", None),
        ),
        out_specs=(P(("rows", "cols"), None), P("cols", None), P("rows", None, None)),
        check_vma=False,
    )
```

time: 214 us -> 71 us (0.33)
  waiting for transfers between devices: 177 us -> 0 us
  Pallas kernels: 0 us -> 64.6 us
  between operations: 14.6 us -> 1.29 us
  matrix products: 9.16 us -> 0 us
  local copies, waits for them, and re-layouts: 9.95 us -> 5 us
  other arithmetic: 2.97 us -> 0 us
    psum x2 -> x0, waiting for transfers between devices: 105 us -> none  [the longest x1 53.9 us: local(): gram = lax.psum(local_gram, 'cols') / (RB_DEV * 128)]
    pallas_call x0 -> x1, Pallas kernels: none -> 64.6 us  [local(): pl.pallas_call(functools.partial(kernel, n_rows, n_cols, slots), out_shap...]
    reduce_scatter x1 -> x0, waiting for transfers between devices: 44 us -> none  [local(): lax.psum_scatter(partial_value, 'cols', scatter_dimension=0, tiled=True)]
    all_gather x1 -> x0, waiting for transfers between devices: 27.4 us -> none  [local(): y_panel = lax.all_gather(y_shard, 'cols', axis=0, tiled=True)]
    dot_general x5 -> x0, matrix products: 9.16 us -> none  [the longest x1 3.03 us: local(): jnp.dot(y_shard.T, y_shard, precision=high, preferred_element_type=jnp.fl...]
    dot_general x4 -> x0, local copies, waits for them, and re-layouts: 4.84 us -> none  [the longest x1 2.57 us: local(): jnp.einsum('sr,sak->rak', row_onehot, products, precision=high)]
    gather x2 -> x0, local copies, waits for them, and re-layouts: 2.82 us -> none  [the longest x1 2.2 us: local(): y_tiles = y_panel.reshape(RB_DEV, 128, test_cols)[rows_local]]
    unnamed x9 -> x5, local copies, waits for them, and re-layouts: 2.29 us -> 5 us
  transfers between devices with their start and end apart: 4 -> 0, of which waited for: 4 -> 0; matrix products, arithmetic and copies ran while one was open for 6% -> 0% of each run, Pallas kernels for 0% -> 0%
where the time goes in v3:
time: 71 us; the launch traced here: 70.8 us
  Pallas kernels  64.6 us (91%)
  local copies, waits for them, and re-layouts  5 us (7%)
  between operations  1.29 us (2%)
    pallas_call x1, Pallas kernels, local(): pl.pallas_call(functools.partial(kernel, n_rows, n_cols, slots), out_shap...  64.6 us
    unnamed x5, local copies, waits for them, and re-layouts  5 us

profile of v3, /device:TPU:0, one launch (start us, length us, event | category | flops | bytes accessed | tf_op | source)
XLA Modules:
  0.0 70.8 jit_solution(18215117554883961566)
XLA Ops:
  1.3 64.6 %shard_map.76 = (f32[128,512]{1,0:T(8,128)}, f32[512,512]{1,0:T(8,128)}, f32[1,512,512]{2,1,0:T(8,128)}) custom-call(s32[1,1,4]{2,1,0:T(1,128)} %rows_ref.1, s32[1,1,4]{2,1,0:T(1,128)} %cols_ref.1, s32[1,1]{1,0:T(1,128)S(6)} %copy.11.live_ref, bf16[1,1,4,128,128]{4,3,2,1,0:T(8,128)(2,1)} %tiles_ref.1, f32[512,512]{1,0:T(8,128)} %om_ref.1), custom_call_target="tpu_custom_call" | custom-call | flops 4000000000 | bytes 4000000 | tf_op jit(solution)/shard_map/pallas_call | solution.py:346
  65.8 1.7 %copy.12 = f32[128,512]{1,0:T(8,128)} copy(f32[128,512]{1,0:T(8,128)} %get-tuple-element.6) | data formatting | bytes 524288
  67.5 0.0 copy-start
  67.5 2.4 %copy.13 = f32[512,512]{1,0:T(8,128)} copy(f32[512,512]{1,0:T(8,128)} %get-tuple-element.7) | data formatting | bytes 2097152
  69.9 0.0 copy-done
  69.9 1.0 %copy.14 = f32[1,512,512]{2,1,0:T(8,128)} copy(f32[1,512,512]{2,1,0:T(8,128)S(1)} %copy-done) | data formatting | bytes 2097152
Async XLA Ops:
  67.5 2.4 %copy-start = (f32[1,512,512]{2,1,0:T(8,128)S(1)}, f32[1,512,512]{2,1,0:T(8,128)}, u32[]{:S(2)}) copy-start(f32[1,512,512]{2,1,0:T(8,128)} %get-tuple-element.8) | copy-start | bytes 3145732

commit v4 on v3

--- a/solution.py
+++ b/solution.py
@@ -258,19 +258,33 @@
     place(sib_codes, sib_tiles, a_mat, ctx, a_rows, CB_DEV, row_code)
     partial_sample(0)
     send_sample(0)
+    partial_sample(1)
+    send_sample(1)
     for s in range(slots):
         tile_t[s] = tiles_f[s].T
     place(codes, tile_t, a_t, 0, CB_DEV, RB_DEV, lambda i, j: j * CB_DEV + i)
-    if chunks > 1:
-        partial_sample(1)
     reduce_sample(0)
-    if chunks > 1:
-        send_sample(1)
-    if chunks > 2:
-        partial_sample(2)
+    partial_sample(2)
+    send_sample(2)
+    reduce_sample(1)
+    partial_sample(3)
+    send_sample(3)
     swap_sample(0)
     finish_sample(0)
 
+    between = {
+        (0, 1): lambda: reduce_sample(2),
+        (0, 2): lambda: swap_sample(1),
+        (0, 3): lambda: (reduce_sample(3), finish_sample(1)),
+        (1, 0): lambda: gram_rows(0),
+        (1, 1): lambda: swap_sample(2),
+        (1, 2): lambda: gram_rows(1),
+        (1, 3): lambda: finish_sample(2),
+        (2, 0): lambda: swap_sample(3),
+        (2, 1): lambda: gram_rows(2),
+        (2, 3): lambda: finish_sample(3),
+        (3, 1): lambda: gram_rows(3),
+    }
     late = []
     for q in range(chunks):
         for i in range(pieces):
@@ -278,18 +292,8 @@
             late.append((q, i))
             if len(late) > LAG:
                 finish_piece(*late.pop(0))
-            if i == 0 and q + 1 < chunks:
-                reduce_sample(q + 1)
-                if q + 2 < chunks:
-                    send_sample(q + 2)
-            if i == 1:
-                gram_rows(q)
-                if q + 3 < chunks:
-                    partial_sample(q + 3)
-            if i == 2 and q + 1 < chunks:
-                swap_sample(q + 1)
-        if q + 1 < chunks:
-            finish_sample(q + 1)
+            if (q, i) in between:
+                between[q, i]()
     for item in late:
         finish_piece(*item)
 

time: 71 us -> 69.5 us (0.979)
  Pallas kernels: 64.6 us -> 63 us
    pallas_call x1, Pallas kernels: 64.6 us -> 63 us  [local(): pl.pallas_call(functools.partial(kernel, n_rows, n_cols, slots), out_shap...]
where the time goes in v4:
time: 69.5 us; the launch traced here: 69.3 us
  Pallas kernels  63 us (91%)
  local copies, waits for them, and re-layouts  5 us (7%)
  between operations  1.29 us (2%)
    pallas_call x1, Pallas kernels, local(): pl.pallas_call(functools.partial(kernel, n_rows, n_cols, slots), out_shap...  63 us
    unnamed x5, local copies, waits for them, and re-layouts  5 us

profile of v4, /device:TPU:0, one launch (start us, length us, event | category | flops | bytes accessed | tf_op | source)
XLA Modules:
  0.0 69.3 jit_solution(12947567971391501737)
XLA Ops:
  1.3 63.0 %shard_map.76 = (f32[128,512]{1,0:T(8,128)}, f32[512,512]{1,0:T(8,128)}, f32[1,512,512]{2,1,0:T(8,128)}) custom-call(s32[1,1,4]{2,1,0:T(1,128)} %rows_ref.1, s32[1,1,4]{2,1,0:T(1,128)} %cols_ref.1, s32[1,1]{1,0:T(1,128)S(6)} %copy.11.live_ref, bf16[1,1,4,128,128]{4,3,2,1,0:T(8,128)(2,1)} %tiles_ref.1, f32[512,512]{1,0:T(8,128)} %om_ref.1), custom_call_target="tpu_custom_call" | custom-call | flops 4000000000 | bytes 4000000 | tf_op jit(solution)/shard_map/pallas_call | solution.py:350
  64.3 1.7 %copy.12 = f32[128,512]{1,0:T(8,128)} copy(f32[128,512]{1,0:T(8,128)} %get-tuple-element.6) | data formatting | bytes 524288
  65.9 0.0 copy-start
  65.9 2.4 %copy.13 = f32[512,512]{1,0:T(8,128)} copy(f32[512,512]{1,0:T(8,128)} %get-tuple-element.7) | data formatting | bytes 2097152
  68.3 0.0 copy-done
  68.3 1.0 %copy.14 = f32[1,512,512]{2,1,0:T(8,128)} copy(f32[1,512,512]{2,1,0:T(8,128)S(1)} %copy-done) | data formatting | bytes 2097152
Async XLA Ops:
  65.9 2.4 %copy-start = (f32[1,512,512]{2,1,0:T(8,128)S(1)}, f32[1,512,512]{2,1,0:T(8,128)}, u32[]{:S(2)}) copy-start(f32[1,512,512]{2,1,0:T(8,128)} %get-tuple-element.8) | copy-start | bytes 3145732

commit v5 on v4

--- a/solution.py
+++ b/solution.py
@@ -13,7 +13,8 @@
 MESH = pl.DeviceIdType.MESH
 F32 = jnp.float32
 BF16 = jnp.bfloat16
-LAG = 1
+LAG = 5
+PIECE = 64
 
 
 def split2(x):
@@ -42,7 +43,7 @@
     share = panel // n_cols
     compact = share == B
     chunks = om_ref.shape[1] // B
-    pieces = ctx // B
+    pieces = ctx // PIECE
     mid = n_rows // 2
     lower = r < mid
     inner = jnp.where(lower, r + 1, r - 1)
@@ -210,39 +211,44 @@
         for j in range(q):
             g_out[0, lanes(j), lanes(q)] = g[:, lanes(j)].T
 
+    def piece(i):
+        return slice(i * PIECE, (i + 1) * PIECE)
+
     def inward(q, i, center):
         dst = zcross if center else zin
         sem = zx_r if center else zc_r
         return remote(
-            zpart.at[q, lanes(i), :], dst.at[q, lanes(i), :], zc_s.at[q, i], sem.at[q, i], (inner, c)
+            zpart.at[q, piece(i), :], dst.at[q, piece(i), :], zc_s.at[q, i], sem.at[q, i], (inner, c)
         )
 
     def outward(q, i):
-        piece = z_out.at[lanes(i), lanes(q)]
-        return remote(piece, piece, zt_s.at[q, i], zt_r.at[q, i], (outer, c))
+        part = z_out.at[piece(i), lanes(q)]
+        return remote(part, part, zt_s.at[q, i], zt_r.at[q, i], (outer, c))
 
     def onward(q, i):
-        piece = z_out.at[lanes(i), lanes(q)]
-        return remote(piece, piece, zf_s.at[q, i], zt_r.at[q, i], (outer, c))
+        part = z_out.at[piece(i), lanes(q)]
+        return remote(part, part, zf_s.at[q, i], zt_r.at[q, i], (outer, c))
 
     def finish_piece(q, i):
         @pl.when(is_center)
         def _():
             inward(q, i, True).wait_recv()
-            z_out[lanes(i), lanes(q)] = zpart[q, lanes(i), :] + zcross[q, lanes(i), :]
+            z_out[piece(i), lanes(q)] = zpart[q, piece(i), :] + zcross[q, piece(i), :]
 
             @pl.when(has_outer)
             def _():
                 outward(q, i).start()
 
     def chain_piece(q, i):
-        both = jnp.dot(a_t[lanes(i), :], y2[q], preferred_element_type=F32)
-        zpart[q, lanes(i), :] = both[:, :B] + both[:, B:]
+        if i % (B // PIECE) == 0:
+            rows = lanes(i * PIECE // B)
+            both = jnp.dot(a_t[rows, :], y2[q], preferred_element_type=F32)
+            zpart[q, rows, :] = both[:, :B] + both[:, B:]
 
         @pl.when(has_outer)
         def _():
             inward(q, i, False).wait_recv()
-            zpart[q, lanes(i), :] += zin[q, lanes(i), :]
+            zpart[q, piece(i), :] += zin[q, piece(i), :]
 
         @pl.when(is_center)
         def _():
@@ -267,23 +273,24 @@
     partial_sample(2)
     send_sample(2)
     reduce_sample(1)
+    swap_sample(0)
     partial_sample(3)
     send_sample(3)
-    swap_sample(0)
     finish_sample(0)
 
     between = {
         (0, 1): lambda: reduce_sample(2),
-        (0, 2): lambda: swap_sample(1),
-        (0, 3): lambda: (reduce_sample(3), finish_sample(1)),
-        (1, 0): lambda: gram_rows(0),
-        (1, 1): lambda: swap_sample(2),
-        (1, 2): lambda: gram_rows(1),
-        (1, 3): lambda: finish_sample(2),
-        (2, 0): lambda: swap_sample(3),
-        (2, 1): lambda: gram_rows(2),
-        (2, 3): lambda: finish_sample(3),
-        (3, 1): lambda: gram_rows(3),
+        (0, 3): lambda: swap_sample(1),
+        (0, 5): lambda: reduce_sample(3),
+        (0, 7): lambda: finish_sample(1),
+        (1, 1): lambda: gram_rows(0),
+        (1, 2): lambda: swap_sample(2),
+        (1, 4): lambda: gram_rows(1),
+        (1, 7): lambda: finish_sample(2),
+        (2, 1): lambda: swap_sample(3),
+        (2, 3): lambda: gram_rows(2),
+        (2, 7): lambda: finish_sample(3),
+        (3, 3): lambda: gram_rows(3),
     }
     late = []
     for q in range(chunks):
@@ -340,7 +347,7 @@
         m = n_cols // 2
         panel, ctx = RB_DEV * B, CB_DEV * B
         chunks = test_cols // B
-        pieces = ctx // B
+        pieces = ctx // PIECE
         share = panel // n_cols
         used = m * B if share == B else panel
         vmem = pl.BlockSpec(memory_space=pltpu.VMEM)

time: 69.5 us -> 65.4 us (0.941)
  Pallas kernels: 63 us -> 58.9 us
    pallas_call x1, Pallas kernels: 63 us -> 58.9 us  [local(): pl.pallas_call(functools.partial(kernel, n_rows, n_cols, slots), out_shap...]
where the time goes in v5:
time: 65.4 us; the launch traced here: 65.2 us
  Pallas kernels  58.9 us (90%)
  local copies, waits for them, and re-layouts  5 us (8%)
  between operations  1.29 us (2%)
    pallas_call x1, Pallas kernels, local(): pl.pallas_call(functools.partial(kernel, n_rows, n_cols, slots), out_shap...  58.9 us
    unnamed x5, local copies, waits for them, and re-layouts  5 us

profile of v5, /device:TPU:0, one launch (start us, length us, event | category | flops | bytes accessed | tf_op | source)
XLA Modules:
  0.0 65.2 jit_solution(16883771566075516328)
XLA Ops:
  1.3 58.9 %shard_map.76 = (f32[128,512]{1,0:T(8,128)}, f32[512,512]{1,0:T(8,128)}, f32[1,512,512]{2,1,0:T(8,128)}) custom-call(s32[1,1,4]{2,1,0:T(1,128)} %rows_ref.1, s32[1,1,4]{2,1,0:T(1,128)} %cols_ref.1, s32[1,1]{1,0:T(1,128)S(6)} %copy.11.live_ref, bf16[1,1,4,128,128]{4,3,2,1,0:T(8,128)(2,1)} %tiles_ref.1, f32[512,512]{1,0:T(8,128)} %om_ref.1), custom_call_target="tpu_custom_call" | custom-call | flops 4000000000 | bytes 4000000 | tf_op jit(solution)/shard_map/pallas_call | solution.py:357
  60.2 1.7 %copy.12 = f32[128,512]{1,0:T(8,128)} copy(f32[128,512]{1,0:T(8,128)} %get-tuple-element.6) | data formatting | bytes 524288
  61.8 0.0 copy-start
  61.8 2.4 %copy.13 = f32[512,512]{1,0:T(8,128)} copy(f32[512,512]{1,0:T(8,128)} %get-tuple-element.7) | data formatting | bytes 2097152
  64.2 0.0 copy-done
  64.2 1.0 %copy.14 = f32[1,512,512]{2,1,0:T(8,128)} copy(f32[1,512,512]{2,1,0:T(8,128)S(1)} %copy-done) | data formatting | bytes 2097152
Async XLA Ops:
  61.8 2.4 %copy-start = (f32[1,512,512]{2,1,0:T(8,128)S(1)}, f32[1,512,512]{2,1,0:T(8,128)}, u32[]{:S(2)}) copy-start(f32[1,512,512]{2,1,0:T(8,128)} %get-tuple-element.8) | copy-start | bytes 3145732

commit v6 on v5

--- a/solution.py
+++ b/solution.py
@@ -26,9 +26,9 @@
     n_rows, n_cols, slots,
     rows_ref, cols_ref, live_ref, tiles_ref, om_ref,
     y_out, z_out, g_out,
-    codes, sib_codes, tiles_in, tiles_f, sib_tiles, tile_t, om_in, sib_om, om2, a_mat, a_t,
-    ypart, rs_recv, ypanel, y2, yhi, ylo, zpart, zin, zcross,
-    load_s, init_s, init_r, om_s, om_r, rs_s, rs_r, ag_s, ag_r, sb_s, sb_r,
+    codes, tiles_in, tiles_f, tile_t, om_in, om2, a_mat, a_t,
+    ypart, xrecv, rs_recv, ypanel, y2, yhi, ylo, zpart, zin, zcross,
+    load_s, xs_s, xs_r, rs_s, rs_r, ag_s, ag_r, sb_s, sb_r,
     zc_s, zc_r, zx_r, zt_s, zt_r, zf_s,
 ):
     r = lax.axis_index("rows")
@@ -99,18 +99,6 @@
         codes[s] = jnp.full((8, B), code, jnp.int32)
         tiles_f[s] = tiles_in[s].astype(F32)
 
-    pl.semaphore_wait(barrier, 1 + (m - 1) + (n_rows - 1))
-
-    init = (
-        remote(tiles_f, sib_tiles, init_s.at[0], init_r.at[0], (r, sib)),
-        remote(codes, sib_codes, init_s.at[1], init_r.at[1], (r, sib)),
-    )
-    om_swap = [
-        remote(om_ref.at[:, lanes(q)], sib_om.at[q], om_s.at[q], om_r.at[q], (r, sib)) for q in range(chunks)
-    ]
-    for cp in (*init, *om_swap):
-        cp.start()
-
     def place(code_ref, source, target, col0, rows, cols, want):
         def line(i, _):
             for j in range(cols):
@@ -126,18 +114,22 @@
 
         lax.fori_loop(0, rows, line, 0)
 
-    def place_om(q, src, row0):
-        hi, lo = split2(src[q])
-        om2[q, row0 : row0 + ctx, 0:B] = hi
-        om2[q, row0 : row0 + ctx, B : 2 * B] = lo
-
     if compact:
-        a_rows, row_code = m, lambda i, j: (2 * i + core) * CB_DEV + j
+
+        def row_code(i, j):
+            parity = jnp.where(i < m, other, core)
+            return (2 * lax.rem(i, m) + parity) * CB_DEV + j
+
     else:
-        a_rows, row_code = RB_DEV, lambda i, j: i * CB_DEV + j
-
-    def part_rows(j):
-        start = j * share if compact else (2 * j + core) * share
+
+        def row_code(i, j):
+            return i * CB_DEV + j
+
+    def part_rows(j, mine):
+        if compact:
+            start = (j + (m if mine else 0)) * share
+        else:
+            start = (2 * j + (core if mine else other)) * share
         return pl.ds(pl.multiple_of(start, 8), share)
 
     def panel_rows(j, parity):
@@ -146,7 +138,7 @@
     def rs_copy(q, d):
         j = lax.rem(chip + d, m)
         return remote(
-            ypart.at[q, part_rows(j), :], rs_recv.at[q, d - 1], rs_s.at[q, d - 1], rs_r.at[q, d - 1],
+            ypart.at[q, part_rows(j, True), :], rs_recv.at[q, d - 1], rs_s.at[q, d - 1], rs_r.at[q, d - 1],
             (r, j * 2 + core),
         )
 
@@ -159,23 +151,39 @@
         block = ypanel.at[q, panel_rows(lax.rem(chip + m - d, m), core), :]
         return remote(block, block, sb_s.at[q, d], sb_r.at[q, d], (r, sib))
 
+    def xs_copy(q, d):
+        j = lax.rem(chip + d, m)
+        return remote(
+            ypart.at[q, part_rows(j, False), :], xrecv.at[q, d], xs_s.at[q, d], xs_r.at[q, d], (r, sib)
+        )
+
     def partial_sample(q):
         load_om[q].wait()
-        place_om(q, om_in, 0)
-        om_swap[q].wait_recv()
-        place_om(q, sib_om, ctx)
+        hi, lo = split2(om_in[q])
+        om2[q, :, 0:B] = hi
+        om2[q, :, B : 2 * B] = lo
         step = 2 * B
-        for k in range(a_rows * B // step):
+        for k in range(panel // step):
             rows = slice(k * step, (k + 1) * step)
             both = jnp.dot(a_mat[rows, :], om2[q], preferred_element_type=F32)
             ypart[q, rows, :] = both[:, :B] + both[:, B:]
 
+    def swap_partial(q):
+        each_chip(lambda d: xs_copy(q, d).start())
+        xs_copy(q, 0).start()
+
     def send_sample(q):
-        each_chip(lambda d: rs_copy(q, d).start())
+        def step(d):
+            xs_copy(q, d).wait_recv()
+            ypart[q, part_rows(lax.rem(chip + d, m), True), :] += xrecv[q, d]
+            rs_copy(q, d).start()
+
+        each_chip(step)
 
     def reduce_sample(q):
+        xs_copy(q, 0).wait_recv()
+        total = ypart[q, part_rows(chip, True), :] + xrecv[q, 0]
         each_chip(lambda d: rs_copy(q, d).wait_recv())
-        total = ypart[q, part_rows(chip), :]
         for d in range(m - 1):
             total = total + rs_recv[q, d]
         ypanel[q, panel_rows(chip, core), :] = total
@@ -258,27 +266,29 @@
         def _():
             inward(q, i, False).start()
 
-    place(codes, tiles_f, a_mat, 0, a_rows, CB_DEV, row_code)
-    for cp in init:
-        cp.wait_recv()
-    place(sib_codes, sib_tiles, a_mat, ctx, a_rows, CB_DEV, row_code)
+    place(codes, tiles_f, a_mat, 0, RB_DEV, CB_DEV, row_code)
     partial_sample(0)
+    pl.semaphore_wait(barrier, 1 + (m - 1) + (n_rows - 1))
+    swap_partial(0)
+    partial_sample(1)
+    swap_partial(1)
     send_sample(0)
-    partial_sample(1)
-    send_sample(1)
     for s in range(slots):
         tile_t[s] = tiles_f[s].T
     place(codes, tile_t, a_t, 0, CB_DEV, RB_DEV, lambda i, j: j * CB_DEV + i)
+    send_sample(1)
     reduce_sample(0)
     partial_sample(2)
+    swap_partial(2)
+    reduce_sample(1)
     send_sample(2)
-    reduce_sample(1)
     swap_sample(0)
     partial_sample(3)
-    send_sample(3)
+    swap_partial(3)
     finish_sample(0)
 
     between = {
+        (0, 0): lambda: send_sample(3),
         (0, 1): lambda: reduce_sample(2),
         (0, 3): lambda: swap_sample(1),
         (0, 5): lambda: reduce_sample(3),
@@ -317,9 +327,9 @@
                 def _():
                     onward(q, i).start()
 
-    for cp in (*init, *om_swap):
-        cp.wait_send()
     for q in range(chunks):
+        xs_copy(q, 0).wait_send()
+        each_chip(lambda d: xs_copy(q, d).wait_send())
         each_chip(lambda d: rs_copy(q, d).wait_send())
         each_chip(lambda d: ag_copy(q, d).wait_send())
         sb_copy(q, 0).wait_send()
@@ -349,7 +359,6 @@
         chunks = test_cols // B
         pieces = ctx // PIECE
         share = panel // n_cols
-        used = m * B if share == B else panel
         vmem = pl.BlockSpec(memory_space=pltpu.VMEM)
         smem = pl.BlockSpec(memory_space=pltpu.SMEM)
         hbm = pl.BlockSpec(memory_space=pltpu.HBM)
@@ -365,17 +374,15 @@
             out_specs=(vmem, vmem, vmem),
             scratch_shapes=[
                 pltpu.VMEM((slots, 8, B), jnp.int32),
-                pltpu.VMEM((slots, 8, B), jnp.int32),
                 pltpu.VMEM((slots, B, B), BF16),
                 pltpu.VMEM((slots, B, B), F32),
                 pltpu.VMEM((slots, B, B), F32),
-                pltpu.VMEM((slots, B, B), F32),
                 pltpu.VMEM((chunks, ctx, B), F32),
-                pltpu.VMEM((chunks, ctx, B), F32),
-                pltpu.VMEM((chunks, 2 * ctx, 2 * B), BF16),
-                pltpu.VMEM((used, 2 * ctx), BF16),
+                pltpu.VMEM((chunks, ctx, 2 * B), BF16),
+                pltpu.VMEM((panel, ctx), BF16),
                 pltpu.VMEM((ctx, panel), BF16),
-                pltpu.VMEM((chunks, used, B), F32),
+                pltpu.VMEM((chunks, panel, B), F32),
+                pltpu.VMEM((chunks, m, share, B), F32),
                 pltpu.VMEM((chunks, m - 1, share, B), F32),
                 pltpu.VMEM((chunks, panel, B), F32),
                 pltpu.VMEM((chunks, panel, 2 * B), BF16),
@@ -385,8 +392,7 @@
                 pltpu.VMEM((chunks, ctx, B), F32),
                 pltpu.VMEM((chunks, ctx, B), F32),
                 dma((1 + chunks,)),
-                dma((2,)), dma((2,)),
-                dma((chunks,)), dma((chunks,)),
+                dma((chunks, m)), dma((chunks, m)),
                 dma((chunks, m - 1)), dma((chunks, m - 1)),
                 dma((chunks, m - 1)), dma((chunks, m - 1)),
                 dma((chunks, m)), dma((chunks, m)),
@@ -394,7 +400,7 @@
                 dma((chunks, pieces)), dma((chunks, pieces)), dma((chunks, pieces)),
             ],
             compiler_params=pltpu.CompilerParams(
-                collective_id=0, has_side_effects=True, vmem_limit_bytes=60 * 1024 * 1024
+                collective_id=0, has_side_effects=True, vmem_limit_bytes=51 * 1024 * 1024
             ),
             cost_estimate=pl.CostEstimate(flops=4_000_000_000, bytes_accessed=4_000_000, transcendentals=0),
         )(tile_rows, tile_cols, live_counts, tile_values, test_block)

time: 65.4 us -> 61.3 us (0.937)
  Pallas kernels: 58.9 us -> 56.3 us
  local copies, waits for them, and re-layouts: 5 us -> 3.55 us
    pallas_call x1, Pallas kernels: 58.9 us -> 56.3 us  [local(): pl.pallas_call(functools.partial(kernel, n_rows, n_cols, slots), out_shap...]
    unnamed x5 -> x9, local copies, waits for them, and re-layouts: 5 us -> 3.55 us
where the time goes in v6:
time: 61.3 us; the launch traced here: 61.2 us
  Pallas kernels  56.3 us (92%)
  local copies, waits for them, and re-layouts  3.55 us (6%)
  between operations  1.34 us (2%)
    pallas_call x1, Pallas kernels, local(): pl.pallas_call(functools.partial(kernel, n_rows, n_cols, slots), out_shap...  56.3 us
    unnamed x9, local copies, waits for them, and re-layouts  3.55 us

profile of v6, /device:TPU:0, one launch (start us, length us, event | category | flops | bytes accessed | tf_op | source)
XLA Modules:
  0.0 61.2 jit_solution(6176846672031511815)
XLA Ops:
  0.6 0.0 copy-start.2
  0.6 0.0 copy-start.1
  1.3 0.0 copy-done.2
  1.3 0.0 copy-done.1
  1.3 0.0 copy-start
  1.3 0.9 %copy-done = bf16[1,1,4,128,128]{4,3,2,1,0:T(8,128)(2,1)S(1)} copy-done((bf16[1,1,4,128,128]{4,3,2,1,0:T(8,128)(2,1)S(1)}, bf16[1,1,4,128,128]{4,3,2,1,0:T(8,128)(2,1)}, u32[]{:S(2)}) %copy-start) | copy-done | bytes 131096
  2.2 56.3 %shard_map.76 = (f32[128,512]{1,0:T(8,128)S(1)}, f32[512,512]{1,0:T(8,128)S(1)}, f32[1,512,512]{2,1,0:T(8,128)S(1)}) custom-call(s32[1,1,4]{2,1,0:T(1,128)S(1)} %copy-done.1, s32[1,1,4]{2,1,0:T(1,128)S(1)} %copy-done.2, s32[1,1]{1,0:T(1,128)S(6)} %copy.11.live_ref, bf16[1,1,4,128,128]{4,3,2,1,0:T(8,128)(2,1)S(1)} %copy-done, f32[512,512]{1,0:T(8,128)} %om_ref.1), custom_call_target="tpu_custom_call" | custom-call | flops 4000000000 | bytes 4000000 | tf_op jit(solution)/shard_map/pallas_call | solution.py:366
  58.5 0.7 %copy.12 = f32[128,512]{1,0:T(8,128)} copy(f32[128,512]{1,0:T(8,128)S(1)} %get-tuple-element.6) | data formatting | bytes 524288
  59.2 1.0 %copy.13 = f32[512,512]{1,0:T(8,128)} copy(f32[512,512]{1,0:T(8,128)S(1)} %get-tuple-element.7) | data formatting | bytes 2097152
  60.2 1.0 %copy.14 = f32[1,512,512]{2,1,0:T(8,128)} copy(f32[1,512,512]{2,1,0:T(8,128)S(1)} %get-tuple-element.8) | data formatting | bytes 2097152
Async XLA Ops:
  0.6 0.7 %copy-start.2 = (s32[1,1,4]{2,1,0:T(1,128)S(1)}, s32[1,1,4]{2,1,0:T(1,128)}, u32[]{:S(2)}) copy-start(s32[1,1,4]{2,1,0:T(1,128)} %cols_ref.1) | copy-start | bytes 52
  0.6 0.7 %copy-start.1 = (s32[1,1,4]{2,1,0:T(1,128)S(1)}, s32[1,1,4]{2,1,0:T(1,128)}, u32[]{:S(2)}) copy-start(s32[1,1,4]{2,1,0:T(1,128)} %rows_ref.1) | copy-start | bytes 52
  1.3 0.9 %copy-start = (bf16[1,1,4,128,128]{4,3,2,1,0:T(8,128)(2,1)S(1)}, bf16[1,1,4,128,128]{4,3,2,1,0:T(8,128)(2,1)}, u32[]{:S(2)}) copy-start(bf16[1,1,4,128,128]{4,3,2,1,0:T(8,128)(2,1)} %tiles_ref.1) | copy-start | bytes 393220

commit v7 on v6

--- a/solution.py
+++ b/solution.py
@@ -27,7 +27,7 @@
     rows_ref, cols_ref, live_ref, tiles_ref, om_ref,
     y_out, z_out, g_out,
     codes, tiles_in, tiles_f, tile_t, om_in, om2, a_mat, a_t,
-    ypart, xrecv, rs_recv, ypanel, y2, yhi, ylo, zpart, zin, zcross,
+    ypart, xrecv, rs_recv, ypanel, y2, zpart, zin, zcross,
     load_s, xs_s, xs_r, rs_s, rs_r, ag_s, ag_r, sb_s, sb_r,
     zc_s, zc_r, zx_r, zt_s, zt_r, zf_s,
 ):
@@ -202,22 +202,20 @@
         sb_copy(q, 0).wait_recv()
         each_chip(lambda d: sb_copy(q, d).wait_recv())
         hi, lo = split2(ypanel[q])
-        y2[q, :, 0:B] = hi
-        y2[q, :, B : 2 * B] = lo
-        yhi[:, lanes(q)] = hi
-        ylo[:, lanes(q)] = lo
+        y2[:, 2 * q * B : (2 * q + 1) * B] = hi
+        y2[:, (2 * q + 1) * B : (2 * q + 2) * B] = lo
 
     def gram_rows(q):
         dims = (((0,), (0,)), ((), ()))
-        upto = slice(0, (q + 1) * B)
-        hi_q, lo_q = yhi[:, lanes(q)], ylo[:, lanes(q)]
-        g = lax.dot_general(hi_q, yhi[:, upto], dims, preferred_element_type=F32)
-        g += lax.dot_general(hi_q, ylo[:, upto], dims, preferred_element_type=F32)
-        g += lax.dot_general(lo_q, yhi[:, upto], dims, preferred_element_type=F32)
-        g = g * (1.0 / (RB_DEV * B))
-        g_out[0, lanes(q), upto] = g
-        for j in range(q):
-            g_out[0, lanes(j), lanes(q)] = g[:, lanes(j)].T
+        own = slice(2 * q * B, (2 * q + 2) * B)
+        parts = lax.dot_general(y2[:, own], y2[:, : own.stop], dims, preferred_element_type=F32)
+        both = parts[:B, :] + parts[B:, :]
+        for j in range(q + 1):
+            g = both[:, 2 * j * B : (2 * j + 1) * B] + both[:, (2 * j + 1) * B : (2 * j + 2) * B]
+            g = g * (1.0 / (RB_DEV * B))
+            g_out[0, lanes(q), lanes(j)] = g
+            if j < q:
+                g_out[0, lanes(j), lanes(q)] = g.T
 
     def piece(i):
         return slice(i * PIECE, (i + 1) * PIECE)
@@ -250,7 +248,7 @@
     def chain_piece(q, i):
         if i % (B // PIECE) == 0:
             rows = lanes(i * PIECE // B)
-            both = jnp.dot(a_t[rows, :], y2[q], preferred_element_type=F32)
+            both = jnp.dot(a_t[rows, :], y2[:, 2 * q * B : (2 * q + 2) * B], preferred_element_type=F32)
             zpart[q, rows, :] = both[:, :B] + both[:, B:]
 
         @pl.when(has_outer)
@@ -293,14 +291,10 @@
         (0, 3): lambda: swap_sample(1),
         (0, 5): lambda: reduce_sample(3),
         (0, 7): lambda: finish_sample(1),
-        (1, 1): lambda: gram_rows(0),
         (1, 2): lambda: swap_sample(2),
-        (1, 4): lambda: gram_rows(1),
         (1, 7): lambda: finish_sample(2),
         (2, 1): lambda: swap_sample(3),
-        (2, 3): lambda: gram_rows(2),
         (2, 7): lambda: finish_sample(3),
-        (3, 3): lambda: gram_rows(3),
     }
     late = []
     for q in range(chunks):
@@ -313,6 +307,8 @@
                 between[q, i]()
     for item in late:
         finish_piece(*item)
+    for q in range(chunks):
+        gram_rows(q)
 
     for q in range(chunks):
         for i in range(pieces):
@@ -385,9 +381,7 @@
                 pltpu.VMEM((chunks, m, share, B), F32),
                 pltpu.VMEM((chunks, m - 1, share, B), F32),
                 pltpu.VMEM((chunks, panel, B), F32),
-                pltpu.VMEM((chunks, panel, 2 * B), BF16),
-                pltpu.VMEM((panel, test_cols), BF16),
-                pltpu.VMEM((panel, test_cols), BF16),
+                pltpu.VMEM((panel, 2 * test_cols), BF16),
                 pltpu.VMEM((chunks, ctx, B), F32),
                 pltpu.VMEM((chunks, ctx, B), F32),
                 pltpu.VMEM((chunks, ctx, B), F32),

time: 61.3 us -> 61.3 us (level)
  no operation moved by 1% of the time
where the time goes in v7:
time: 61.3 us; the launch traced here: 61.1 us
  Pallas kernels  56.2 us (92%)
  local copies, waits for them, and re-layouts  3.55 us (6%)
  between operations  1.34 us (2%)
    pallas_call x1, Pallas kernels, local(): pl.pallas_call(functools.partial(kernel, n_rows, n_cols, slots), out_shap...  56.2 us
    unnamed x9, local copies, waits for them, and re-layouts  3.55 us

profile of v7, /device:TPU:0, one launch (start us, length us, event | category | flops | bytes accessed | tf_op | source)
XLA Modules:
  0.0 61.1 jit_solution(8752893486650160814)
XLA Ops:
  0.6 0.0 copy-start.2
  0.6 0.0 copy-start.1
  1.3 0.0 copy-done.2
  1.3 0.0 copy-done.1
  1.3 0.0 copy-start
  1.3 0.9 %copy-done = bf16[1,1,4,128,128]{4,3,2,1,0:T(8,128)(2,1)S(1)} copy-done((bf16[1,1,4,128,128]{4,3,2,1,0:T(8,128)(2,1)S(1)}, bf16[1,1,4,128,128]{4,3,2,1,0:T(8,128)(2,1)}, u32[]{:S(2)}) %copy-start) | copy-done | bytes 131096
  2.2 56.2 %shard_map.76 = (f32[128,512]{1,0:T(8,128)S(1)}, f32[512,512]{1,0:T(8,128)S(1)}, f32[1,512,512]{2,1,0:T(8,128)S(1)}) custom-call(s32[1,1,4]{2,1,0:T(1,128)S(1)} %copy-done.1, s32[1,1,4]{2,1,0:T(1,128)S(1)} %copy-done.2, s32[1,1]{1,0:T(1,128)S(6)} %copy.11.live_ref, bf16[1,1,4,128,128]{4,3,2,1,0:T(8,128)(2,1)S(1)} %copy-done, f32[512,512]{1,0:T(8,128)} %om_ref.1), custom_call_target="tpu_custom_call" | custom-call | flops 4000000000 | bytes 4000000 | tf_op jit(solution)/shard_map/pallas_call | solution.py:362
  58.5 0.7 %copy.12 = f32[128,512]{1,0:T(8,128)} copy(f32[128,512]{1,0:T(8,128)S(1)} %get-tuple-element.6) | data formatting | bytes 524288
  59.2 1.0 %copy.13 = f32[512,512]{1,0:T(8,128)} copy(f32[512,512]{1,0:T(8,128)S(1)} %get-tuple-element.7) | data formatting | bytes 2097152
  60.1 1.0 %copy.14 = f32[1,512,512]{2,1,0:T(8,128)} copy(f32[1,512,512]{2,1,0:T(8,128)S(1)} %get-tuple-element.8) | data formatting | bytes 2097152
Async XLA Ops:
  0.6 0.7 %copy-start.2 = (s32[1,1,4]{2,1,0:T(1,128)S(1)}, s32[1,1,4]{2,1,0:T(1,128)}, u32[]{:S(2)}) copy-start(s32[1,1,4]{2,1,0:T(1,128)} %cols_ref.1) | copy-start | bytes 52
  0.6 0.7 %copy-start.1 = (s32[1,1,4]{2,1,0:T(1,128)S(1)}, s32[1,1,4]{2,1,0:T(1,128)}, u32[]{:S(2)}) copy-start(s32[1,1,4]{2,1,0:T(1,128)} %rows_ref.1) | copy-start | bytes 52
  1.3 0.9 %copy-start = (bf16[1,1,4,128,128]{4,3,2,1,0:T(8,128)(2,1)S(1)}, bf16[1,1,4,128,128]{4,3,2,1,0:T(8,128)(2,1)}, u32[]{:S(2)}) copy-start(bf16[1,1,4,128,128]{4,3,2,1,0:T(8,128)(2,1)} %tiles_ref.1) | copy-start | bytes 393220

commit v8 on v7

--- a/solution.py
+++ b/solution.py
@@ -99,7 +99,7 @@
         codes[s] = jnp.full((8, B), code, jnp.int32)
         tiles_f[s] = tiles_in[s].astype(F32)
 
-    def place(code_ref, source, target, col0, rows, cols, want):
+    def place(code_ref, source, target, first, end, cols, want):
         def line(i, _):
             for j in range(cols):
                 code = want(i, j)
@@ -107,12 +107,12 @@
                 for s in range(slots):
                     hit = jnp.broadcast_to((code_ref[s] == code)[None], val.shape)
                     val = jnp.where(hit, source[s].reshape(val.shape), val)
-                target[pl.ds(pl.multiple_of(i * B, B), B), col0 + j * B : col0 + (j + 1) * B] = (
+                target[pl.ds(pl.multiple_of(i * B, B), B), j * B : (j + 1) * B] = (
                     val.reshape(B, B).astype(BF16)
                 )
             return 0
 
-        lax.fori_loop(0, rows, line, 0)
+        lax.fori_loop(first, end, line, 0)
 
     if compact:
 
@@ -157,16 +157,22 @@
             ypart.at[q, part_rows(j, False), :], xrecv.at[q, d], xs_s.at[q, d], xs_r.at[q, d], (r, sib)
         )
 
-    def partial_sample(q):
+    def load_block(q):
         load_om[q].wait()
         hi, lo = split2(om_in[q])
         om2[q, :, 0:B] = hi
         om2[q, :, B : 2 * B] = lo
+
+    def partial_rows(q, first, end):
         step = 2 * B
-        for k in range(panel // step):
+        for k in range(first * B // step, end * B // step):
             rows = slice(k * step, (k + 1) * step)
             both = jnp.dot(a_mat[rows, :], om2[q], preferred_element_type=F32)
             ypart[q, rows, :] = both[:, :B] + both[:, B:]
+
+    def partial_sample(q):
+        load_block(q)
+        partial_rows(q, 0, RB_DEV)
 
     def swap_partial(q):
         each_chip(lambda d: xs_copy(q, d).start())
@@ -264,10 +270,14 @@
         def _():
             inward(q, i, False).start()
 
-    place(codes, tiles_f, a_mat, 0, RB_DEV, CB_DEV, row_code)
-    partial_sample(0)
+    first = RB_DEV // 2 if compact else RB_DEV
+    load_block(0)
+    place(codes, tiles_f, a_mat, 0, first, CB_DEV, row_code)
+    partial_rows(0, 0, first)
     pl.semaphore_wait(barrier, 1 + (m - 1) + (n_rows - 1))
     swap_partial(0)
+    place(codes, tiles_f, a_mat, first, RB_DEV, CB_DEV, row_code)
+    partial_rows(0, first, RB_DEV)
     partial_sample(1)
     swap_partial(1)
     send_sample(0)
@@ -291,9 +301,12 @@
         (0, 3): lambda: swap_sample(1),
         (0, 5): lambda: reduce_sample(3),
         (0, 7): lambda: finish_sample(1),
+        (1, 1): lambda: gram_rows(0),
         (1, 2): lambda: swap_sample(2),
+        (1, 5): lambda: gram_rows(1),
         (1, 7): lambda: finish_sample(2),
         (2, 1): lambda: swap_sample(3),
+        (2, 5): lambda: gram_rows(2),
         (2, 7): lambda: finish_sample(3),
     }
     late = []
@@ -307,8 +320,7 @@
                 between[q, i]()
     for item in late:
         finish_piece(*item)
-    for q in range(chunks):
-        gram_rows(q)
+    gram_rows(3)
 
     for q in range(chunks):
         for i in range(pieces):

time: 61.3 us -> 61.4 us (level)
  no operation moved by 1% of the time
where the time goes in v8:
time: 61.4 us; the launch traced here: 61.2 us
  Pallas kernels  56.3 us (92%)
  local copies, waits for them, and re-layouts  3.55 us (6%)
  between operations  1.34 us (2%)
    pallas_call x1, Pallas kernels, local(): pl.pallas_call(functools.partial(kernel, n_rows, n_cols, slots), out_shap...  56.3 us
    unnamed x9, local copies, waits for them, and re-layouts  3.55 us

profile of v8, /device:TPU:0, one launch (start us, length us, event | category | flops | bytes accessed | tf_op | source)
XLA Modules:
  0.0 61.2 jit_solution(5190216172268388340)
XLA Ops:
  0.6 0.0 copy-start.2
  0.6 0.0 copy-start.1
  1.3 0.0 copy-done.2
  1.3 0.0 copy-done.1
  1.3 0.0 copy-start
  1.3 0.9 %copy-done = bf16[1,1,4,128,128]{4,3,2,1,0:T(8,128)(2,1)S(1)} copy-done((bf16[1,1,4,128,128]{4,3,2,1,0:T(8,128)(2,1)S(1)}, bf16[1,1,4,128,128]{4,3,2,1,0:T(8,128)(2,1)}, u32[]{:S(2)}) %copy-start) | copy-done | bytes 131096
  2.2 56.3 %shard_map.76 = (f32[128,512]{1,0:T(8,128)S(1)}, f32[512,512]{1,0:T(8,128)S(1)}, f32[1,512,512]{2,1,0:T(8,128)S(1)}) custom-call(s32[1,1,4]{2,1,0:T(1,128)S(1)} %copy-done.1, s32[1,1,4]{2,1,0:T(1,128)S(1)} %copy-done.2, s32[1,1]{1,0:T(1,128)S(6)} %copy.11.live_ref, bf16[1,1,4,128,128]{4,3,2,1,0:T(8,128)(2,1)S(1)} %copy-done, f32[512,512]{1,0:T(8,128)} %om_ref.1), custom_call_target="tpu_custom_call" | custom-call | flops 4000000000 | bytes 4000000 | tf_op jit(solution)/shard_map/pallas_call | solution.py:374
  58.6 0.7 %copy.12 = f32[128,512]{1,0:T(8,128)} copy(f32[128,512]{1,0:T(8,128)S(1)} %get-tuple-element.6) | data formatting | bytes 524288
  59.3 1.0 %copy.13 = f32[512,512]{1,0:T(8,128)} copy(f32[512,512]{1,0:T(8,128)S(1)} %get-tuple-element.7) | data formatting | bytes 2097152
  60.3 1.0 %copy.14 = f32[1,512,512]{2,1,0:T(8,128)} copy(f32[1,512,512]{2,1,0:T(8,128)S(1)} %get-tuple-element.8) | data formatting | bytes 2097152
Async XLA Ops:
  0.6 0.7 %copy-start.2 = (s32[1,1,4]{2,1,0:T(1,128)S(1)}, s32[1,1,4]{2,1,0:T(1,128)}, u32[]{:S(2)}) copy-start(s32[1,1,4]{2,1,0:T(1,128)} %cols_ref.1) | copy-start | bytes 52
  0.6 0.7 %copy-start.1 = (s32[1,1,4]{2,1,0:T(1,128)S(1)}, s32[1,1,4]{2,1,0:T(1,128)}, u32[]{:S(2)}) copy-start(s32[1,1,4]{2,1,0:T(1,128)} %rows_ref.1) | copy-start | bytes 52
  1.3 0.9 %copy-start = (bf16[1,1,4,128,128]{4,3,2,1,0:T(8,128)(2,1)S(1)}, bf16[1,1,4,128,128]{4,3,2,1,0:T(8,128)(2,1)}, u32[]{:S(2)}) copy-start(bf16[1,1,4,128,128]{4,3,2,1,0:T(8,128)(2,1)} %tiles_ref.1) | copy-start | bytes 393220
